TPU v7x, 32 devices: a whole 2x2x4 slice. The times are simulated.
32 devices in a mesh: lat: 16 (over z, y, core), lon: 2 (over x).
Axes of the slice: x: 2, y: 2, z: 4, core: 2. Of those that a mesh axis runs over, the one named last changes fastest.
Arguments:
- source_field: bfloat16 [384, 768, 384], P('lat', 'lon'), may hold values from -6 to 6
- cotangent: bfloat16 [384, 768, 384], P('lat', 'lon'), may hold values from -6 to 6
- weight: bfloat16 [3, 384, 384], replicated, may hold values from -0.1875 to 0.1875
- spectral_gain: float32 [384, 384], replicated, may hold values from 0.1 to 1.9
- legendre: bfloat16 [384, 384, 384], P(('lat', 'lon')), may hold values from -0.3125 to 0.3125
- support_lat: int32 [384, 16], replicated, may hold values from -2 to 2
- support_lon: int32 [384, 16], replicated, may hold values from -4 to 4
- support_val: float32 [384, 16, 3], replicated, may hold values from -1.5 to 1.5
- order_map: int32 [384], replicated, may hold values from 0 to 383, each once
Outputs:
- result: bfloat16 [384, 768, 384], P('lat', 'lon')
- grad_input: bfloat16 [384, 768, 384], P('lat', 'lon')
- grad_weight: float32 [3, 384, 384], replicated
- grad_gain: float32 [384, 384], replicated
Inputs may be any that keep to these rules, and one draw needn't show every extreme that they name: `order_map`: each order appears once.
All inputs are finite; a program needn't handle non-finite values.
Results may differ from a plain program's by a relative error of at most 0.009.
Values may be sent and summed in bfloat16 or wider, within the bound.
A program may use at most 512 MiB of HBM per device.

v0:
```python
import math

import jax
import jax.numpy as jnp
from jax import lax
from jax.experimental import pallas as pl
from jax.experimental.pallas import tpu as pltpu
from jax.sharding import PartitionSpec as P

NLON = 768
M = 384
K = 3
H = 2
DW = 4


SQRT_HALF = 0.7071067811865476
INV_SQRT_TAU = 0.3989422804014327


def extended(block, sides, width, periodic):
    for axis, dim in sides:
        count = lax.axis_size(axis)
        forward = [(i, i + 1) for i in range(count - 1)]
        if periodic:
            forward.append((count - 1, 0))
        backward = [(target, source) for source, target in forward]
        low = lax.ppermute(
            lax.slice_in_dim(block, block.shape[dim] - width, None, axis=dim), axis, forward
        )
        high = lax.ppermute(lax.slice_in_dim(block, 0, width, axis=dim), axis, backward)
        block = jnp.concatenate([low, block, high], axis=dim)
    return block


def gelu_value(values):
    return 0.5 * values * (1.0 + lax.erf(values * SQRT_HALF))


def gelu_slope(values):
    return 0.5 * (1.0 + lax.erf(values * SQRT_HALF)) + values * INV_SQRT_TAU * jnp.exp(
        -0.5 * values * values
    )


def tap_table(support_lat, support_lon, support_val):
    lat_steps = jnp.arange(2 * H + 1, dtype=jnp.int32) - H
    lon_steps = jnp.arange(2 * DW + 1, dtype=jnp.int32) - DW
    lat_onehot = (support_lat[:, :, None] == lat_steps[None, None, :]).astype(jnp.float32)
    lon_onehot = (support_lon[:, :, None] == lon_steps[None, None, :]).astype(jnp.float32)
    return jnp.einsum(
        "tsk,tsa,tsd->tkad", support_val, lat_onehot, lon_onehot, precision=lax.Precision.HIGHEST
    )


def dft_table(order_map):
    frequency = jnp.repeat(order_map, 2)
    component = jnp.arange(frequency.shape[0], dtype=jnp.int32) % 2
    longitude = jnp.arange(NLON, dtype=jnp.int32)
    cycles = longitude[:, None] * frequency[None, :] % NLON
    angles = cycles.astype(jnp.float32) * (2.0 * math.pi / NLON)
    matrix = jnp.where(component[None, :] == 0, jnp.cos(angles), -jnp.sin(angles)) * math.sqrt(
        2.0 / NLON
    )
    return matrix.astype(jnp.bfloat16)


P_BLOCK = 96
Q_BLOCK = 128
N_LAT_TAPS = 2 * H + 1


def tap_coefficients(tap_rows, row_count, mirror):
    coef_list = []
    for place in range(N_LAT_TAPS):
        if mirror:
            taken = tap_rows[place : place + row_count, :, N_LAT_TAPS - 1 - place, ::-1]
        else:
            taken = tap_rows[H : H + row_count, :, place, :]
        coef_list.append(taken)
    coefs = jnp.stack(coef_list, axis=2).reshape(row_count, K * N_LAT_TAPS, 2 * DW + 1)
    return jnp.pad(coefs, ((0, 0), (0, 1), (0, Q_BLOCK - 2 * DW - 1)))


def fill_taps(coef_ref, window_refs, band_ref, taps_ref):
    for k in range(K):
        for place in range(N_LAT_TAPS):
            index = k * N_LAT_TAPS + place
            row = jnp.broadcast_to(coef_ref[0, index : index + 1, :], (P_BLOCK, Q_BLOCK))
            band = pltpu.roll(row, 0, 1, stride=1, stride_axis=0)
            band_ref[
                k * P_BLOCK : (k + 1) * P_BLOCK, place * Q_BLOCK : (place + 1) * Q_BLOCK
            ] = band.astype(jnp.bfloat16)
    col_count, wide = taps_ref.shape
    chan_count = wide // K
    for start in range(0, col_count, P_BLOCK):
        window = jnp.concatenate([ref[0, start : start + Q_BLOCK, :] for ref in window_refs], axis=0)
        summed = jnp.dot(band_ref[...], window, preferred_element_type=jnp.float32)
        for k in range(K):
            taps_ref[start : start + P_BLOCK, k * chan_count : (k + 1) * chan_count] = summed[
                k * P_BLOCK : (k + 1) * P_BLOCK
            ].astype(jnp.bfloat16)


def conv_kernel(coef_ref, w0, w1, w2, w3, w4, weight_ref, conv_ref, band_ref, taps_ref):
    fill_taps(coef_ref, (w0, w1, w2, w3, w4), band_ref, taps_ref)
    conv_ref[0] = jnp.dot(
        taps_ref[...], weight_ref[...], preferred_element_type=jnp.float32
    ).astype(jnp.bfloat16)


def back_kernel(
    coef_ref, w0, w1, w2, w3, w4, weight_ref, source_ref, input_ref, weight_grad_ref, band_ref, taps_ref
):
    fill_taps(coef_ref, (w0, w1, w2, w3, w4), band_ref, taps_ref)
    input_ref[0] = jnp.dot(
        taps_ref[...], weight_ref[...], preferred_element_type=jnp.float32
    ).astype(jnp.bfloat16)

    @pl.when(pl.program_id(0) == 0)
    def _():
        weight_grad_ref[...] = jnp.zeros_like(weight_grad_ref)

    weight_grad_ref[...] += lax.dot_general(
        source_ref[0], taps_ref[...], (((0,), (0,)), ((), ())), preferred_element_type=jnp.float32
    )


def tap_call(kernel, padded, coefs, flat_weight, col_count, source=None):
    row_count = coefs.shape[0]
    wide_count, chan_count = padded.shape[1:]

    def window_spec(place):
        return pl.BlockSpec((1, wide_count, chan_count), lambda t: (t + place, 0, 0))

    row_spec = pl.BlockSpec((1, col_count, chan_count), lambda t: (t, 0, 0))
    in_specs = [pl.BlockSpec((1,) + coefs.shape[1:], lambda t: (t, 0, 0))]
    in_specs += [window_spec(place) for place in range(N_LAT_TAPS)]
    in_specs += [pl.BlockSpec(flat_weight.shape, lambda t: (0, 0))]
    operands = [coefs] + [padded] * N_LAT_TAPS + [flat_weight]
    row_shape = jax.ShapeDtypeStruct((row_count, col_count, chan_count), jnp.bfloat16)
    positions = row_count * col_count
    flops = 2 * positions * chan_count * K * (N_LAT_TAPS * Q_BLOCK + chan_count)
    if source is None:
        out_specs, out_shape = row_spec, row_shape
    else:
        in_specs.append(row_spec)
        operands.append(source)
        grad_shape = (chan_count, K * chan_count)
        out_specs = (row_spec, pl.BlockSpec(grad_shape, lambda t: (0, 0)))
        out_shape = (row_shape, jax.ShapeDtypeStruct(grad_shape, jnp.float32))
        flops += 2 * positions * chan_count * K * chan_count
    return pl.pallas_call(
        kernel,
        grid=(row_count,),
        in_specs=in_specs,
        out_specs=out_specs,
        out_shape=out_shape,
        scratch_shapes=[
            pltpu.VMEM((K * P_BLOCK, N_LAT_TAPS * Q_BLOCK), jnp.bfloat16),
            pltpu.VMEM((col_count, K * chan_count), jnp.bfloat16),
        ],
        compiler_params=pltpu.CompilerParams(vmem_limit_bytes=48 * 1024 * 1024),
        cost_estimate=pl.CostEstimate(
            flops=flops, bytes_accessed=2 * 8 * positions * chan_count, transcendentals=0
        ),
    )(*operands)


def padded_field(field):
    lon_padded = extended(field, (("lon", 1),), DW, True)
    lon_padded = jnp.pad(lon_padded, ((0, 0), (0, Q_BLOCK - P_BLOCK - 2 * DW), (0, 0)))
    return extended(lon_padded, (("lat", 0),), H, False)


def to_lines(field):
    count = lax.axis_size("lon")
    parts = field.reshape((count, field.shape[0] // count) + field.shape[1:])
    return lax.all_to_all(parts, "lon", split_axis=0, concat_axis=0, tiled=True)


def to_grid(parts):
    moved = lax.all_to_all(parts, "lon", split_axis=0, concat_axis=0, tiled=True)
    return moved.reshape((-1,) + parts.shape[2:])


def to_spec(field):
    count = lax.axis_size("lat") * lax.axis_size("lon")
    rows, cols, chans = field.shape
    parts = field.reshape(rows, count, cols // count, chans).transpose(1, 0, 2, 3)
    moved = lax.all_to_all(parts, ("lat", "lon"), split_axis=0, concat_axis=0, tiled=True)
    return moved.reshape(count * rows, cols // count, chans)


def to_line_rows(field):
    count = lax.axis_size("lat") * lax.axis_size("lon")
    rows, cols, chans = field.shape
    parts = field.reshape(count, rows // count, cols, chans)
    moved = lax.all_to_all(parts, ("lat", "lon"), split_axis=0, concat_axis=0, tiled=True)
    return moved.transpose(1, 0, 2, 3).reshape(rows // count, count * cols, chans)


def legendre_in(spectral, table_rows):
    lat_total, col_total, chan_total = spectral.shape
    halves = spectral.reshape(lat_total, col_total // 2, 2, chan_total)
    return jnp.einsum("olt,toqc->olqc", table_rows, halves, preferred_element_type=jnp.float32)


def legendre_out(coefficients, table_rows):
    synthesis = jnp.einsum(
        "olt,olqc->toqc", table_rows, coefficients, preferred_element_type=jnp.float32
    )
    lat_total, order_count, two_parts, chan_total = synthesis.shape
    return synthesis.reshape(lat_total, order_count * two_parts, chan_total)


def body(
    source_field,
    cotangent,
    weight,
    spectral_gain,
    legendre,
    support_lat,
    support_lon,
    support_val,
    order_map,
):
    row_count, col_count, chan_count = source_field.shape
    lon_devices = lax.axis_size("lon")
    lat_total = row_count * lax.axis_size("lat")
    band_index = lax.axis_index("lat")
    block_index = lax.axis_index("lon")
    tap_weights = tap_table(support_lat, support_lon, support_val)
    tap_pad = jnp.pad(tap_weights, ((H, H), (0, 0), (0, 0), (0, 0)))
    tap_rows = lax.dynamic_slice_in_dim(tap_pad, band_index * row_count, row_count + 2 * H, 0)
    dft_matrix = dft_table(order_map)
    dft_parts = dft_matrix.reshape(lon_devices, col_count, dft_matrix.shape[1])
    flat_weight = weight.reshape(K * chan_count, chan_count)
    flat_weight_back = weight.transpose(0, 2, 1).reshape(K * chan_count, chan_count)
    all_rows = jnp.arange(lat_total, dtype=jnp.int32).astype(jnp.float32)
    quad_all = jnp.sin(math.pi * (all_rows + 0.5) / lat_total)
    line_rows = row_count // lon_devices
    line_quad = lax.dynamic_slice_in_dim(
        quad_all, band_index * row_count + block_index * line_rows, line_rows, 0
    )
    cot_line_spec = jnp.einsum(
        "nrpc,npj->rjc", to_lines(cotangent), dft_parts, preferred_element_type=jnp.float32
    )
    cot_spectral = to_spec(cot_line_spec.astype(jnp.bfloat16))
    conv_out = tap_call(
        conv_kernel,
        padded_field(source_field),
        tap_coefficients(tap_rows, row_count, False),
        flat_weight,
        col_count,
    )
    conv_wide = conv_out.astype(jnp.float32)
    hidden = gelu_value(conv_wide).astype(jnp.bfloat16)
    line_spec = jnp.einsum(
        "nrpc,npj->rjc", to_lines(hidden), dft_parts, preferred_element_type=jnp.float32
    )
    spectral = to_spec((line_spec * line_quad[:, None, None]).astype(jnp.bfloat16))
    cot_coefficients = legendre_in(cot_spectral, legendre)
    cot_filtered = (spectral_gain[None, :, None, :] * cot_coefficients).astype(jnp.bfloat16)
    cot_synth = legendre_out(cot_filtered, legendre)
    cot_synth = (cot_synth * quad_all[:, None, None]).astype(jnp.bfloat16)
    cot_synth_lines = to_line_rows(cot_synth)
    coefficients = legendre_in(spectral, legendre)
    gain_part = jnp.sum(coefficients * cot_coefficients, axis=(0, 2))
    filtered = (spectral_gain[None, :, None, :] * coefficients).astype(jnp.bfloat16)
    synth_lines = to_line_rows(legendre_out(filtered, legendre).astype(jnp.bfloat16))
    cot_hidden = jnp.einsum(
        "rjc,npj->nrpc", cot_synth_lines, dft_parts, preferred_element_type=jnp.float32
    ).astype(jnp.bfloat16)
    cot_hidden_grid = to_grid(cot_hidden)
    cot_conv = (
        cotangent.astype(jnp.float32) + cot_hidden_grid.astype(jnp.float32) * gelu_slope(conv_wide)
    ).astype(jnp.bfloat16)
    grad_input, weight_part = tap_call(
        back_kernel,
        padded_field(cot_conv),
        tap_coefficients(tap_rows, row_count, True),
        flat_weight_back,
        col_count,
        source_field,
    )
    branch = jnp.einsum(
        "rjc,npj->nrpc", synth_lines, dft_parts, preferred_element_type=jnp.float32
    ).astype(jnp.bfloat16)
    result = (conv_wide + to_grid(branch).astype(jnp.float32)).astype(jnp.bfloat16)
    weight_total = lax.psum(weight_part, ("lat", "lon")).reshape(chan_count, K, chan_count)
    gain_total = lax.psum(gain_part, ("lat", "lon"))
    grad_weight = weight_total.transpose(1, 0, 2) / math.sqrt(1.0 * lat_total * NLON)
    grad_gain = gain_total / math.sqrt(2.0 * M)
    return (result, grad_input, grad_weight, grad_gain)


def solution(mesh):
    return jax.shard_map(
        body,
        mesh=mesh,
        in_specs=(
            P("lat", "lon", None),
            P("lat", "lon", None),
            P(),
            P(),
            P(("lat", "lon"), None, None),
            P(),
            P(),
            P(),
            P(),
        ),
        out_specs=(P("lat", "lon", None), P("lat", "lon", None), P(), P()),
        check_vma=False,
    )
```

profile of v0, /device:TPU:13, one launch (start us, length us, event | category | flops | bytes accessed | tf_op | source)
XLA Modules:
  0.0 1352.1 jit_solution(7807345597457461757)
XLA Ops:
  49.4 40.9 %shard_map.120 = bf16[24,384,384]{2,1,0:T(8,128)(2,1)} custom-call(f32[24,16,128]{2,1,0:T(8,128)S(1)} %pad.19.coef_ref, bf16[28,416,384]{2,1,0:T(8,128)(2,1)} %pad_maximum_fusion.w0.w1.w2.w3.w4, bf16[28,416,384]{2,1,0:T(8,128)(2,1)} %pad_maximum_fusion.w0.w1.w2.w3.w4, bf16[28,416,384]{2,1,0:T(8,128)(2,1)} %pad_maximum_fusion.w0.w1.w2.w3.w4, ...), custom_call_target="tpu_custom_call" | custom-call | flops 21743271936 | bytes 56623104 | tf_op jit(solution)/shard_map/pallas_call | solution.py:153
  106.7 73.5 %all-to-all-done = bf16[2,12,384,384]{3,2,1,0:T(8,128)(2,1)} async-done(((bf16[2,12,384,384]{3,2,1,0:T(8,128)(2,1)}), bf16[2,12,384,384]{3,2,1,0:T(8,128)(2,1)}, u32[]{:S(2)}, u32[]{:S(2)}) %all-to-all-start) | async-done | bytes 7077920 | tf_op jit(solution)/shard_map/all_to_all | solution.py:179
  187.0 18.3 %fusion.17 = bf16[768,12,384]{2,0,1:T(8,128)(2,1)S(1)} fusion(bf16[2,12,384,384]{3,2,1,0:T(8,128)(2,1)} %all-to-all-done, f32[12]{0:T(128)S(1)} %dynamic_slice.7, s32[768]{0:T(1024)S(1)} %mul.135, s32[2,384]{1,0:T(2,128)S(1)} %multiply_add_fusion, pred[768]{0:T(1024)(128)(4,1)S(1)} %fusion.75), kind=kOutput, calls=%fused_computation.26 | convolution fusion | flops 5450563584 | bytes 14162736 | tf_op jit(solution)/shard_map/nrpc,npj->rjc/dot_general | solution.py:259
  208.9 52.6 %all-to-all-done.4 = bf16[2,12,384,384]{3,2,1,0:T(8,128)(2,1)} async-done(((bf16[2,12,384,384]{3,2,1,0:T(8,128)(2,1)}), bf16[2,12,384,384]{3,2,1,0:T(8,128)(2,1)}, u32[]{:S(2)}, u32[]{:S(2)}) %all-to-all-start.4) | async-done | bytes 7077920 | tf_op jit(solution)/shard_map/all_to_all | solution.py:179
  261.6 10.4 all-to-all-start.1
  272.0 18.2 %bitcast_convert_fusion = bf16[768,12,384]{2,0,1:T(8,128)(2,1)S(1)} fusion(bf16[2,12,384,384]{3,2,1,0:T(8,128)(2,1)} %all-to-all-done.4, s32[768]{0:T(1024)S(1)} %mul.135, s32[2,384]{1,0:T(2,128)S(1)} %multiply_add_fusion, pred[768]{0:T(1024)(128)(4,1)S(1)} %fusion.75), kind=kOutput, calls=%fused_computation.24 | convolution fusion | flops 5447024640 | bytes 14162688 | tf_op jit(solution)/shard_map/nrpc,npj->rjc/dot_general | solution.py:246
  293.9 130.5 %all-to-all-done.1 = bf16[32,12,24,384]{3,2,1,0:T(8,128)(2,1)} async-done(((bf16[32,12,24,384]{3,2,1,0:T(8,128)(2,1)}), bf16[32,12,24,384]{3,2,1,0:T(8,128)(2,1)}, u32[]{:S(2)}, u32[]{:S(2)}) %all-to-all-start.1) | async-done | bytes 7077920 | tf_op jit(solution)/shard_map/all_to_all | solution.py:191
  424.4 10.1 all-to-all-start.5
  436.6 14.7 %reshape_reshape.6 = bf16[384,12,2,384]{3,2,1,0:T(2,128)(2,1)} reshape(bf16[32,12,24,384]{3,2,1,0:T(8,128)(2,1)} %all-to-all-done.1) | data formatting | bytes 14155776 | tf_op jit(solution)/shard_map/reshape;reshape | solution.py:205
  451.3 10.2 fusion.30
  461.5 13.1 convert_bitcast_fusion.2
  474.6 32.7 %copy.102 = bf16[384,12,2,384]{3,2,1,0:T(2,128)(2,1)} copy(bf16[384,12,2,384]{3,0,2,1:T(8,128)(2,1)} %convert_bitcast_fusion.2) | data formatting | bytes 14155776 | tf_op jit(solution)/shard_map/convert_element_type | solution.py:271
  507.2 15.2 %convert_element_type.118 = bf16[32,12,24,384]{3,2,1,0:T(8,128)(2,1)} reshape(bf16[384,12,2,384]{3,2,1,0:T(2,128)(2,1)} %copy.102) | data formatting | bytes 14155776 | tf_op jit(solution)/shard_map/convert_element_type | solution.py:271
  522.5 64.4 %all-to-all-done.5 = bf16[32,12,24,384]{3,2,1,0:T(8,128)(2,1)} async-done(((bf16[32,12,24,384]{3,2,1,0:T(8,128)(2,1)}), bf16[32,12,24,384]{3,2,1,0:T(8,128)(2,1)}, u32[]{:S(2)}, u32[]{:S(2)}) %all-to-all-start.5) | async-done | bytes 7077920 | tf_op jit(solution)/shard_map/all_to_all | solution.py:191
  586.9 9.9 all-to-all-start.2
  596.9 14.7 %reshape_reshape.7 = bf16[384,12,2,384]{3,2,1,0:T(2,128)(2,1)} reshape(bf16[32,12,24,384]{3,2,1,0:T(8,128)(2,1)} %all-to-all-done.5) | data formatting | bytes 14155776 | tf_op jit(solution)/shard_map/reshape;reshape | solution.py:205
  611.6 13.8 %fusion.19 = (f32[384,384]{0,1:T(8,128)}, f32[12,2,384,384]{3,2,1,0:T(8,128)}) fusion(f32[12,2,384,384]{3,2,1,0:T(8,128)} %fusion.30, bf16[12,384,384]{2,1,0:T(8,128)(2,1)S(1)} %copy-done, bf16[384,12,2,384]{3,2,1,0:T(2,128)(2,1)} %reshape_reshape.7), kind=kOutput, calls=%fused_computation.30 | convolution fusion | flops 2724839424 | bytes 39518208 | tf_op jit(solution)/shard_map/olt,toqc->olqc/dot_general | solution.py:206
  625.3 14.7 %convolution_bitcast_fusion = f32[384,12,2,384]{3,0,2,1:T(8,128)} fusion(f32[12,2,384,384]{3,2,1,0:T(8,128)} %get-tuple-element.38, f32[384,384]{0,1:T(8,128)S(1)} %copy-done.7, bf16[12,384,384]{2,1,0:T(8,128)(2,1)S(1)} %copy-done), kind=kOutput, calls=%fused_computation.36 | convolution fusion | flops 2724986880 | bytes 32440320 | tf_op jit(solution)/shard_map/olt,olqc->toqc/dot_general | solution.py:210
  640.0 28.9 %copy.112 = f32[384,12,2,384]{3,2,1,0:T(2,128)} copy(f32[384,12,2,384]{3,0,2,1:T(8,128)} %convolution_bitcast_fusion) | data formatting | bytes 28311552 | tf_op jit(solution)/shard_map/olt,olqc->toqc/transpose | solution.py:210
  668.9 17.4 %reshape.135 = f32[32,12,24,384]{3,2,1,0:T(8,128)} reshape(f32[384,12,2,384]{3,2,1,0:T(2,128)} %copy.112) | data formatting | bytes 28311552 | tf_op jit(solution)/shard_map/reshape | solution.py:214
  686.3 8.9 multiply_convert_fusion
  695.3 53.9 %all-to-all-done.2 = bf16[32,12,24,384]{3,2,1,0:T(8,128)(2,1)} async-done(((bf16[32,12,24,384]{3,2,1,0:T(8,128)(2,1)}), bf16[32,12,24,384]{3,2,1,0:T(8,128)(2,1)}, u32[]{:S(2)}, u32[]{:S(2)}) %all-to-all-start.2) | async-done | bytes 7077920 | tf_op jit(solution)/shard_map/all_to_all | solution.py:199
  749.1 9.9 all-to-all-start.6
  763.3 17.2 %convert_bitcast_fusion.1 = bf16[2,12,384,384]{3,2,1,0:T(8,128)(2,1)} fusion(bf16[12,768,384,1]{2,1,0,3:T(8,128)(2,1)S(1)} %bitcast.127, s32[768]{0:T(1024)S(1)} %copy-done.12, s32[2,384]{1,0:T(2,128)S(1)} %copy-done.14, pred[768]{0:T(1024)(128)(4,1)S(1)} %copy-done.17), kind=kOutput, calls=%fused_computation.49 | convolution fusion | flops 5447024640 | bytes 14162688 | tf_op jit(solution)/shard_map/rjc,npj->nrpc/dot_general | solution.py:287
  780.5 130.9 %all-to-all-done.6 = bf16[32,12,24,384]{3,2,1,0:T(8,128)(2,1)} async-done(((bf16[32,12,24,384]{3,2,1,0:T(8,128)(2,1)}), bf16[32,12,24,384]{3,2,1,0:T(8,128)(2,1)}, u32[]{:S(2)}, u32[]{:S(2)}) %all-to-all-start.6) | async-done | bytes 7077920 | tf_op jit(solution)/shard_map/all_to_all | solution.py:199
  922.3 17.2 %convert_bitcast_fusion = bf16[2,12,384,384]{3,2,1,0:T(8,128)(2,1)} fusion(bf16[12,768,384,1]{2,1,0,3:T(8,128)(2,1)S(1)} %bitcast.124, s32[768]{0:T(1024)S(1)} %copy-done.12, s32[2,384]{1,0:T(2,128)S(1)} %copy-done.14, pred[768]{0:T(1024)(128)(4,1)S(1)} %copy-done.17), kind=kOutput, calls=%fused_computation.48 | convolution fusion | flops 5447024640 | bytes 14162688 | tf_op jit(solution)/shard_map/rjc,npj->nrpc/dot_general | solution.py:272
  939.6 59.2 %all-to-all-done.3 = bf16[2,12,384,384]{3,2,1,0:T(8,128)(2,1)} async-done(((bf16[2,12,384,384]{3,2,1,0:T(8,128)(2,1)}), bf16[2,12,384,384]{3,2,1,0:T(8,128)(2,1)}, u32[]{:S(2)}, u32[]{:S(2)}) %all-to-all-start.3) | async-done | bytes 7077920 | tf_op jit(solution)/shard_map/all_to_all | solution.py:183
  998.7 81.8 %all_to_all.40 = bf16[2,12,384,384]{3,2,1,0:T(8,128)(2,1)S(1)} all-to-all(bf16[2,12,384,384]{3,2,1,0:T(8,128)(2,1)} %convert_bitcast_fusion), channel_id=1, replica_groups=mesh['lat'=16,'lon'=2] {'lon'}, dimensions={0} | all-to-all | bytes 14155776 | tf_op jit(solution)/shard_map/all_to_all | solution.py:183
  1080.5 14.2 %fusion.15 = (bf16[24,384,384]{2,1,0:T(8,128)(2,1)S(1)}, bf16[24,384,384]{2,1,0:T(8,128)(2,1)}) fusion(bf16[24,384,384]{2,1,0:T(8,128)(2,1)} %shard_map.120, bf16[24,384,384]{2,1,0:T(8,128)(2,1)} %param.10, bf16[2,12,384,384]{3,2,1,0:T(8,128)(2,1)S(1)} %all_to_all.40, bf16[2,12,384,384]{3,2,1,0:T(8,128)(2,1)} %all-to-all-done.3), kind=kLoop, calls=%fused_computation.22 | loop fusion | flops 60162048 | bytes 42467328 | tf_op jit(solution)/shard_map/convert_element_type | solution.py:278
  1129.4 7.8 pad_maximum_fusion.1.w0.w1.w2.w3.w4
  1137.3 58.1 %shard_map.121 = (bf16[24,384,384]{2,1,0:T(8,128)(2,1)}, f32[384,1152]{1,0:T(8,128)S(1)}) custom-call(f32[24,16,128]{2,1,0:T(8,128)S(1)} %pad.21.coef_ref, bf16[28,416,384]{2,1,0:T(8,128)(2,1)} %pad_maximum_fusion.1.w0.w1.w2.w3.w4, bf16[28,416,384]{2,1,0:T(8,128)(2,1)} %pad_maximum_fusion.1.w0.w1.w2.w3.w4, ...), custom_call_target="tpu_custom_call" | custom-call | flops 29896998912 | bytes 56623104 | tf_op jit(solution)/shard_map/pallas_call | solution.py:153
  1196.6 135.9 %all-reduce.8.cloned.1.call-done = (f32[384,1152]{1,0:T(8,128)}, f32[384,384]{0,1:T(8,128)}) async-done(((f32[384,1152]{1,0:T(8,128)}, f32[384,384]{0,1:T(8,128)}), (f32[384,1152]{1,0:T(8,128)}, f32[384,384]{0,1:T(8,128)})) %all-reduce.8.cloned.1.call-update) | async-done | bytes 2359312 | tf_op jit(solution)/shard_map/psum | solution.py:291
  (102 shorter events, 138.2 us)
Async XLA Ops:
  7.2 444.2 %copy-start = (bf16[12,384,384]{2,1,0:T(8,128)(2,1)S(1)}, bf16[12,384,384]{2,1,0:T(8,128)(2,1)}, u32[]{:S(2)}) copy-start(bf16[12,384,384]{2,1,0:T(8,128)(2,1)} %param.13) | copy-start | bytes 10616836
  9.0 8.9 collective-permute-start
  10.2 7.7 collective-permute-start.1
  17.9 12.7 copy-start.8
  17.9 12.7 copy-start.9
  17.9 12.7 copy-start.10
  23.0 7.5 copy-start.6
  24.3 15.8 %collective-permute-start.2 = (bf16[2,416,384]{2,1,0:T(8,128)(2,1)}, bf16[2,416,384]{2,1,0:T(8,128)(2,1)}, u32[]{:S(2)}, u32[]{:S(2)}) collective-permute-start(bf16[2,416,384]{2,1,0:T(8,128)(2,1)} %get-tuple-element.24), channel_id=1, source_target_pairs={{0,2},{2,4},{4,6},{6,8},{8,10},{10,12},{12,14},{14,16},{16,18},{18... | collective-permute-start | bytes 1916936 | tf_op jit(solution)/shard_map/ppermute | solution.py:28
  28.6 13.0 collective-permute-start.3
  40.1 9.3 copy-start.2
  98.0 6.7 copy-start.15
  98.0 82.2 %all-to-all-start = ((bf16[2,12,384,384]{3,2,1,0:T(8,128)(2,1)}), bf16[2,12,384,384]{3,2,1,0:T(8,128)(2,1)}, u32[]{:S(2)}, u32[]{:S(2)}) async-start(bf16[2,12,384,384]{3,2,1,0:T(8,128)(2,1)} %bitcast.120), calls=%async_computation | async-start | bytes 14155776 | tf_op jit(solution)/shard_map/all_to_all | solution.py:179
  106.5 165.5 %copy-start.11 = (s32[768]{0:T(1024)}, s32[768]{0:T(1024)S(1)}, u32[]{:S(2)}) copy-start(s32[768]{0:T(1024)S(1)} %mul.135) | copy-start | bytes 9220
  106.7 165.3 %copy-start.16 = (pred[768]{0:T(1024)(128)(4,1)}, pred[768]{0:T(1024)(128)(4,1)S(1)}, u32[]{:S(2)}) copy-start(pred[768]{0:T(1024)(128)(4,1)S(1)} %fusion.75) | copy-start | bytes 2308
  106.7 165.3 %copy-start.13 = (s32[2,384]{1,0:T(2,128)}, s32[2,384]{1,0:T(2,128)S(1)}, u32[]{:S(2)}) copy-start(s32[2,384]{1,0:T(2,128)S(1)} %multiply_add_fusion) | copy-start | bytes 9220
  180.2 81.4 %all-to-all-start.4 = ((bf16[2,12,384,384]{3,2,1,0:T(8,128)(2,1)}), bf16[2,12,384,384]{3,2,1,0:T(8,128)(2,1)}, u32[]{:S(2)}, u32[]{:S(2)}) async-start(bf16[2,12,384,384]{3,2,1,0:T(8,128)(2,1)} %bitcast.123), calls=%async_computation.4 | async-start | bytes 14155776 | tf_op jit(solution)/shard_map/all_to_all | solution.py:179
  261.6 162.8 %all-to-all-start.1 = ((bf16[32,12,24,384]{3,2,1,0:T(8,128)(2,1)}), bf16[32,12,24,384]{3,2,1,0:T(8,128)(2,1)}, u32[]{:S(2)}, u32[]{:S(2)}) async-start(bf16[32,12,24,384]{3,2,1,0:T(8,128)(2,1)} %bitcast.122), calls=%async_computation.1 | async-start | bytes 14155776 | tf_op jit(solution)/shard_map/all_to_all | solution.py:191
  424.4 162.5 %all-to-all-start.5 = ((bf16[32,12,24,384]{3,2,1,0:T(8,128)(2,1)}), bf16[32,12,24,384]{3,2,1,0:T(8,128)(2,1)}, u32[]{:S(2)}, u32[]{:S(2)}) async-start(bf16[32,12,24,384]{3,2,1,0:T(8,128)(2,1)} %bitcast.121), calls=%async_computation.5 | async-start | bytes 14155776 | tf_op jit(solution)/shard_map/all_to_all | solution.py:191
  586.9 162.3 %all-to-all-start.2 = ((bf16[32,12,24,384]{3,2,1,0:T(8,128)(2,1)}), bf16[32,12,24,384]{3,2,1,0:T(8,128)(2,1)}, u32[]{:S(2)}, u32[]{:S(2)}) async-start(bf16[32,12,24,384]{3,2,1,0:T(8,128)(2,1)} %convert_element_type.118), calls=%async_computation.2 | async-start | bytes 14155776 | tf_op jit(solution)/shard_map/all_to_all | solution.py:199
  611.6 13.8 %copy-start.7 = (f32[384,384]{0,1:T(8,128)S(1)}, f32[384,384]{0,1:T(8,128)}, u32[]{:S(2)}) copy-start(f32[384,384]{0,1:T(8,128)} %copy.95) | copy-start | bytes 1769476
  749.1 162.3 %all-to-all-start.6 = ((bf16[32,12,24,384]{3,2,1,0:T(8,128)(2,1)}), bf16[32,12,24,384]{3,2,1,0:T(8,128)(2,1)}, u32[]{:S(2)}, u32[]{:S(2)}) async-start(bf16[32,12,24,384]{3,2,1,0:T(8,128)(2,1)} %multiply_convert_fusion), calls=%async_computation.6 | async-start | bytes 14155776 | tf_op jit(solution)/shard_map/all_to_all | solution.py:199
  759.1 4.2 copy-start.12
  759.1 4.2 copy-start.14
  759.1 4.2 copy-start.17
  911.4 87.3 %all-to-all-start.3 = ((bf16[2,12,384,384]{3,2,1,0:T(8,128)(2,1)}), bf16[2,12,384,384]{3,2,1,0:T(8,128)(2,1)}, u32[]{:S(2)}, u32[]{:S(2)}) async-start(bf16[2,12,384,384]{3,2,1,0:T(8,128)(2,1)} %convert_bitcast_fusion.1), calls=%async_computation.3 | async-start | bytes 14155776 | tf_op jit(solution)/shard_map/all_to_all | solution.py:183
  918.1 414.4 %all-reduce.8.cloned.1.call-start = ((), (), s32[]{:S(2)}) async-start(), calls=%async_computation.8 | async-start | bytes 4718592 | tf_op jit(solution)/shard_map/psum | solution.py:291
  1094.8 3.3 collective-permute-start.4
  1095.2 3.7 collective-permute-start.5
  1101.2 3.0 copy-start.5
  1105.4 24.0 %collective-permute-start.6 = (bf16[2,416,384]{2,1,0:T(8,128)(2,1)}, bf16[2,416,384]{2,1,0:T(8,128)(2,1)}, u32[]{:S(2)}, u32[]{:S(2)}) collective-permute-start(bf16[2,416,384]{2,1,0:T(8,128)(2,1)} %get-tuple-element.22), channel_id=1, source_target_pairs={{0,2},{2,4},{4,6},{6,8},{8,10},{10,12},{12,14},{14,16},{16,18},{18... | collective-permute-start | bytes 1916936 | tf_op jit(solution)/shard_map/ppermute | solution.py:28
  1109.4 20.0 %collective-permute-start.7 = (bf16[2,416,384]{2,1,0:T(8,128)(2,1)}, bf16[2,416,384]{2,1,0:T(8,128)(2,1)}, u32[]{:S(2)}, u32[]{:S(2)}) collective-permute-start(bf16[2,416,384]{2,1,0:T(8,128)(2,1)} %get-tuple-element.23), channel_id=1, source_target_pairs={{2,0},{4,2},{6,4},{8,6},{10,8},{12,10},{14,12},{16,14},{18,16},{20... | collective-permute-start | bytes 1916936 | tf_op jit(solution)/shard_map/ppermute | solution.py:31
  1129.4 7.8 copy-start.3
  (2 other events, 3.4 us)
Sparse Core Ops, SparseCore 0:
  1196.7 135.7 all-reduce.7
where the time goes:
time: 1370 us; the launch traced here: 1350 us
  waiting for transfers between devices  705 us (51%)
  local copies, waits for them, and re-layouts  187 us (14%)
  matrix products  127 us (9%)
  Pallas kernels  99 us (7%)
  blocking collectives  81.8 us (6%)
  starting transfers between devices  76.9 us (6%)
  other arithmetic  61 us (4%)
  between operations  14.7 us (1%)
    all_to_all x2, waiting for transfers between devices, to_spec(): lax.all_to_all(parts, ('lat', 'lon'), split_axis=0, concat_axis=0, tiled=...  195 us
    all_to_all x2, waiting for transfers between devices, to_line_rows(): lax.all_to_all(parts, ('lat', 'lon'), split_axis=0, concat_axis=0, tiled=...  185 us
    psum x1, waiting for transfers between devices, body(): lax.psum(weight_part, ('lat', 'lon')).reshape(chan_count, K, chan_count)  136 us
    all_to_all x2, waiting for transfers between devices, to_lines(): return lax.all_to_all(parts, 'lon', split_axis=0, concat_axis=0, tiled=True)  126 us
    pallas_call x2, Pallas kernels, tap_call(): pl.pallas_call(kernel, grid=(row_count,), in_specs=in_specs, out_specs=ou...  99 us
    all_to_all x1, blocking collectives, to_grid(): lax.all_to_all(parts, 'lon', split_axis=0, concat_axis=0, tiled=True)  81.8 us
    all_to_all x1, waiting for transfers between devices, to_grid(): lax.all_to_all(parts, 'lon', split_axis=0, concat_axis=0, tiled=True)  59.2 us
    convert_element_type x2, local copies, waits for them, and re-layouts, body(): legendre_out(filtered, legendre).astype(jnp.bfloat16)  47.9 us
  transfers between devices with their start and end apart: 16, of which 11 were waited for; matrix products, arithmetic and copies ran while one was open for 23% of the time, Pallas kernels for 0%

commit v1 on v0

v1 whole, which is shorter than its diff:
```python
import functools
import math

import jax
import jax.numpy as jnp
from jax import lax
from jax.experimental import pallas as pl
from jax.experimental.pallas import tpu as pltpu
from jax.sharding import PartitionSpec as P

NLON = 768
M = 384
K = 3
H = 2
DW = 4


SQRT_HALF = 0.7071067811865476
INV_SQRT_TAU = 0.3989422804014327


def gelu_value(values):
    return 0.5 * values * (1.0 + lax.erf(values * SQRT_HALF))


def gelu_slope(values):
    return 0.5 * (1.0 + lax.erf(values * SQRT_HALF)) + values * INV_SQRT_TAU * jnp.exp(
        -0.5 * values * values
    )


def tap_table(support_lat, support_lon, support_val):
    lat_steps = jnp.arange(2 * H + 1, dtype=jnp.int32) - H
    lon_steps = jnp.arange(2 * DW + 1, dtype=jnp.int32) - DW
    lat_onehot = (support_lat[:, :, None] == lat_steps[None, None, :]).astype(jnp.float32)
    lon_onehot = (support_lon[:, :, None] == lon_steps[None, None, :]).astype(jnp.float32)
    return jnp.einsum(
        "tsk,tsa,tsd->tkad", support_val, lat_onehot, lon_onehot, precision=lax.Precision.HIGHEST
    )


def dft_table(longitude, frequency):
    cycles = longitude[:, None] * frequency[None, :] % NLON
    angles = cycles.astype(jnp.float32) * (2.0 * math.pi / NLON)
    matrix = jnp.concatenate([jnp.cos(angles), -jnp.sin(angles)], axis=1) * math.sqrt(2.0 / NLON)
    return matrix.astype(jnp.bfloat16)


P_BLOCK = 96
Q_BLOCK = 128
N_LAT_TAPS = 2 * H + 1
VMEM_LIMIT = 48 * 1024 * 1024
GROUP = 8
LANES = 128


def lane_tiles(wide):
    return [(start, min(LANES, wide - start)) for start in range(0, wide, LANES)]


def wide_scratch(rows, wide):
    return pltpu.VMEM((len(lane_tiles(wide)), rows, LANES), jnp.float32)


def cost(micros):
    return pl.CostEstimate(
        flops=int(micros * 3.3e8), bytes_accessed=int(micros * 1e6), transcendentals=0
    )


def tap_coefficients(tap_rows, row_count, mirror):
    coef_list = []
    for place in range(N_LAT_TAPS):
        if mirror:
            taken = tap_rows[place : place + row_count, :, N_LAT_TAPS - 1 - place, ::-1]
        else:
            taken = tap_rows[H : H + row_count, :, place, :]
        coef_list.append(taken)
    coefs = jnp.stack(coef_list, axis=2).reshape(row_count, K * N_LAT_TAPS, 2 * DW + 1)
    return jnp.pad(coefs, ((0, 0), (0, 1), (0, Q_BLOCK - 2 * DW - 1)))


def fill_taps(coef_ref, window_refs, band_ref, taps_ref):
    for k in range(K):
        for place in range(N_LAT_TAPS):
            index = k * N_LAT_TAPS + place
            row = jnp.broadcast_to(coef_ref[0, index : index + 1, :], (P_BLOCK, Q_BLOCK))
            band = pltpu.roll(row, 0, 1, stride=1, stride_axis=0)
            band_ref[
                k * P_BLOCK : (k + 1) * P_BLOCK, place * Q_BLOCK : (place + 1) * Q_BLOCK
            ] = band.astype(jnp.bfloat16)
    col_count, wide = taps_ref.shape
    chan_count = wide // K
    for start in range(0, col_count, P_BLOCK):
        window = jnp.concatenate([ref[0, start : start + Q_BLOCK, :] for ref in window_refs], axis=0)
        summed = jnp.dot(band_ref[...], window, preferred_element_type=jnp.float32)
        for k in range(K):
            taps_ref[start : start + P_BLOCK, k * chan_count : (k + 1) * chan_count] = summed[
                k * P_BLOCK : (k + 1) * P_BLOCK
            ].astype(jnp.bfloat16)


def pack_row(row, place, place_ref, store):
    count, half, wide = place_ref.shape
    share = wide // 2
    for d in range(count):
        place_ref[d] = jnp.concatenate(
            [row[:half, d * share : (d + 1) * share], row[half:, d * share : (d + 1) * share]], axis=1
        )
    for s in range(count):
        store(s, place_ref[lax.rem(place + s, count)].astype(jnp.bfloat16))


def unpack_row(pieces, place, place_ref):
    count, half, wide = place_ref.shape
    share = wide // 2
    for s in range(count):
        place_ref[lax.rem(place + s, count)] = pieces[s].astype(jnp.float32)
    parts = []
    for d in range(count):
        piece = place_ref[d]
        parts.append(jnp.concatenate([piece[:, :share], piece[:, share:]], axis=0))
    return jnp.concatenate(parts, axis=1)


def pack_kernel(place_ref, row_ref, *refs):
    outs, scratch = refs[:-1], refs[-1]

    def store(s, piece):
        outs[s][0] = piece

    pack_row(row_ref[0].astype(jnp.float32), place_ref[0], scratch, store)


SMEM_SPEC = pl.BlockSpec(memory_space=pltpu.SMEM)


def pack_call(place, field, lon_count, first, count):
    cols, chans = field.shape[1:]
    half, wide = cols // 2, 2 * (chans // lon_count)
    return pl.pallas_call(
        pack_kernel,
        grid=(count,),
        in_specs=[SMEM_SPEC, pl.BlockSpec((1, cols, chans), lambda t: (t + first, 0, 0))],
        out_specs=[pl.BlockSpec((1, half, wide), lambda t: (t, 0, 0))] * lon_count,
        out_shape=[jax.ShapeDtypeStruct((count, half, wide), jnp.bfloat16)] * lon_count,
        scratch_shapes=[pltpu.VMEM((lon_count, half, wide), jnp.float32)],
        compiler_params=pltpu.CompilerParams(vmem_limit_bytes=VMEM_LIMIT),
        cost_estimate=cost(0.6 * count),
    )(place, field)


def conv_kernel(lon_count, place_ref, coef_ref, w0, w1, w2, w3, w4, weight_ref, *refs):
    conv_ref, outs = refs[-4 - lon_count], refs[-3 - lon_count : -3]
    scratch, band_ref, taps_ref = refs[-3:]
    fill_taps(coef_ref, (w0, w1, w2, w3, w4), band_ref, taps_ref)
    conv = jnp.dot(taps_ref[...], weight_ref[...], preferred_element_type=jnp.float32).astype(jnp.bfloat16)
    conv_ref[0] = conv
    hidden = gelu_value(conv.astype(jnp.float32))

    def store(s, piece):
        outs[s][0] = piece

    pack_row(hidden, place_ref[0], scratch, store)


def back_kernel(added, coef_ref, w0, w1, w2, w3, w4, weight_ref, source_ref, *refs):
    input_ref, weight_grad_ref, band_ref, taps_ref = refs[-4:]
    fill_taps(coef_ref, (w0, w1, w2, w3, w4), band_ref, taps_ref)
    input_ref[0] = jnp.dot(
        taps_ref[...], weight_ref[...], preferred_element_type=jnp.float32
    ).astype(jnp.bfloat16)

    @pl.when(pl.program_id(0) == 0)
    def _():
        if added:
            weight_grad_ref[...] = refs[1][...]
        else:
            weight_grad_ref[...] = jnp.zeros_like(weight_grad_ref)

    weight_grad_ref[...] += lax.dot_general(
        source_ref[0], taps_ref[...], (((0,), (0,)), ((), ())), preferred_element_type=jnp.float32
    )


def tap_specs(padded, coefs, flat_weight, first):
    wide_count, chan_count = padded.shape[1:]

    def window_spec(place):
        return pl.BlockSpec((1, wide_count, chan_count), lambda t: (t + first + place, 0, 0))

    in_specs = [pl.BlockSpec((1,) + coefs.shape[1:], lambda t: (t + first, 0, 0))]
    in_specs += [window_spec(place) for place in range(N_LAT_TAPS)]
    in_specs += [pl.BlockSpec(flat_weight.shape, lambda t: (0, 0))]
    return in_specs, [coefs] + [padded] * N_LAT_TAPS + [flat_weight]


def tap_scratch(col_count, chan_count):
    return [
        pltpu.VMEM((K * P_BLOCK, N_LAT_TAPS * Q_BLOCK), jnp.bfloat16),
        pltpu.VMEM((col_count, K * chan_count), jnp.bfloat16),
    ]


def conv_call(place, padded, coefs, flat_weight, col_count, lon_count, first, row_count, held):
    chan_count = padded.shape[2]
    half, wide = col_count // 2, 2 * (chan_count // lon_count)
    in_specs, operands = tap_specs(padded, coefs, flat_weight, first)
    out_specs = [pl.BlockSpec((1, col_count, chan_count), lambda t: (t + first, 0, 0))]
    out_specs += [pl.BlockSpec((1, half, wide), lambda t: (t, 0, 0))] * lon_count
    out_shape = [jax.ShapeDtypeStruct((coefs.shape[0], col_count, chan_count), jnp.bfloat16)]
    aliases = {}
    if held is not None:
        aliases = {len(operands) + 1: 0}
        in_specs.append(pl.BlockSpec(memory_space=pl.ANY))
        operands.append(held)
    out_shape += [jax.ShapeDtypeStruct((row_count, half, wide), jnp.bfloat16)] * lon_count
    outs = pl.pallas_call(
        functools.partial(conv_kernel, lon_count),
        grid=(row_count,),
        in_specs=[SMEM_SPEC] + in_specs,
        out_specs=out_specs,
        out_shape=out_shape,
        scratch_shapes=[pltpu.VMEM((lon_count, half, wide), jnp.float32)]
        + tap_scratch(col_count, chan_count),
        compiler_params=pltpu.CompilerParams(vmem_limit_bytes=VMEM_LIMIT),
        input_output_aliases=aliases,
        cost_estimate=cost(2.0 * row_count),
    )(place, *operands)
    return outs[0], outs[1:]


def back_call(padded, coefs, flat_weight, source, first, row_count, held):
    total_rows, col_count, chan_count = source.shape
    in_specs, operands = tap_specs(padded, coefs, flat_weight, first)
    row_spec = pl.BlockSpec((1, col_count, chan_count), lambda t: (t + first, 0, 0))
    row_shape = jax.ShapeDtypeStruct((total_rows, col_count, chan_count), jnp.bfloat16)
    grad_shape = (chan_count, K * chan_count)
    grad_spec = pl.BlockSpec(grad_shape, lambda t: (0, 0))
    in_specs.append(row_spec)
    operands.append(source)
    aliases = {}
    if held is not None:
        aliases = {len(operands): 0}
        in_specs += [pl.BlockSpec(memory_space=pl.ANY), grad_spec]
        operands += list(held)
    return pl.pallas_call(
        functools.partial(back_kernel, held is not None),
        grid=(row_count,),
        in_specs=in_specs,
        out_specs=(row_spec, grad_spec),
        out_shape=(row_shape, jax.ShapeDtypeStruct(grad_shape, jnp.float32)),
        scratch_shapes=tap_scratch(col_count, chan_count),
        input_output_aliases=aliases,
        compiler_params=pltpu.CompilerParams(vmem_limit_bytes=VMEM_LIMIT),
        cost_estimate=cost(2.4 * row_count),
    )(*operands)


def dft_kernel(scaled, lon_count, starts, table_ref, quad_ref, *refs):
    pieces, out_ref, wide_ref = refs[:-2], refs[-2], refs[-1]
    share = pieces[0].shape[2] // 2
    group, t = pl.program_id(0), pl.program_id(1)
    rows = []
    for s in range(lon_count):
        piece = pieces[s][0]
        for index, start in enumerate(starts):
            piece = jnp.where(group < start, piece, pieces[(index + 1) * lon_count + s][0])
        rows += [piece[:, :share], piece[:, share:]]
    spectrum = jnp.dot(table_ref[...], jnp.concatenate(rows, axis=0), preferred_element_type=jnp.float32)
    orders = spectrum.shape[0] // 2
    lines = jnp.concatenate([spectrum[:orders], spectrum[orders:]], axis=1)
    if scaled:
        lines = lines * quad_ref[0]
    for start, size in lane_tiles(2 * share):
        tile = lines[:, start : start + size]
        if size < LANES:
            tile = jnp.pad(tile, ((0, 0), (0, LANES - size)))
        wide_ref[start // LANES, pl.ds(t, orders, stride=GROUP), :] = tile

    @pl.when(t == GROUP - 1)
    def _():
        blocks, held = out_ref.shape[:2]
        step = held * GROUP
        for b in range(blocks):
            for start, size in lane_tiles(2 * share):
                block = wide_ref[start // LANES, b * step : (b + 1) * step, :size]
                out_ref[b, :, :, start : start + size] = block.reshape(held, GROUP, size).astype(
                    jnp.bfloat16
                )


def dft_call(table, quad_rows, chunks, first, lat_count, scaled):
    lon_count = len(chunks[0])
    half, wide = chunks[0][0].shape[1:]
    held = table.shape[0] // (2 * lat_count)

    def piece_spec(start, count):
        return pl.BlockSpec(
            (1, half, wide), lambda g, t: (jnp.clip(g * GROUP + t - start, 0, count - 1), 0, 0)
        )

    piece_specs, starts, rows = [], [], 0
    for pieces in chunks:
        if rows:
            starts.append(rows // GROUP)
        piece_specs += [piece_spec(rows, pieces[0].shape[0])] * lon_count
        rows += pieces[0].shape[0]
    return pl.pallas_call(
        functools.partial(dft_kernel, scaled, lon_count, starts),
        grid=(rows // GROUP, GROUP),
        in_specs=[
            pl.BlockSpec(table.shape, lambda g, t: (0, 0)),
            pl.BlockSpec((1, 1, wide), lambda g, t: (first + g * GROUP + t, 0, 0)),
        ]
        + piece_specs,
        out_specs=pl.BlockSpec((lat_count, held, GROUP, wide), lambda g, t: (0, 0, g, 0)),
        out_shape=jax.ShapeDtypeStruct((lat_count, held, rows, wide), jnp.bfloat16),
        scratch_shapes=[wide_scratch(lat_count * held * GROUP, wide)],
        compiler_params=pltpu.CompilerParams(vmem_limit_bytes=VMEM_LIMIT),
        cost_estimate=cost(0.9 * rows),
    )(table, quad_rows, *[piece for pieces in chunks for piece in pieces])


def idft_kernel(lon_count, table_ref, wide_in_ref, *refs):
    outs, wide_ref = refs[:lon_count], refs[lon_count]
    wide = wide_in_ref.shape[3]
    t = pl.program_id(1)

    @pl.when(t == 0)
    def _():
        blocks, held = wide_in_ref.shape[:2]
        step = held * GROUP
        for b in range(blocks):
            for start, size in lane_tiles(wide):
                block = wide_in_ref[b, :, :, start : start + size]
                wide_ref[start // LANES, b * step : (b + 1) * step, :size] = block.astype(
                    jnp.float32
                ).reshape(step, size)

    orders = wide_ref.shape[1] // GROUP
    tiles = []
    for start, size in lane_tiles(wide):
        tiles.append(wide_ref[start // LANES, pl.ds(t, orders, stride=GROUP), :][:, :size])
    lines = jnp.concatenate(tiles, axis=1).astype(jnp.bfloat16)
    share = wide // 2
    stacked = jnp.concatenate([lines[:, :share], lines[:, share:]], axis=0)
    grid_rows = jnp.dot(table_ref[...], stacked, preferred_element_type=jnp.float32)
    half = grid_rows.shape[0] // (2 * lon_count)
    for s in range(lon_count):
        start = 2 * s * half
        outs[s][0] = jnp.concatenate(
            [grid_rows[start : start + half], grid_rows[start + half : start + 2 * half]], axis=1
        ).astype(jnp.bfloat16)


def idft_call(table, received, lon_count, first, count):
    lat_count, held, _, wide = received.shape
    start = first // GROUP
    half = table.shape[0] // (2 * lon_count)
    return pl.pallas_call(
        functools.partial(idft_kernel, lon_count),
        grid=(count // GROUP, GROUP),
        in_specs=[
            pl.BlockSpec(table.shape, lambda g, t: (0, 0)),
            pl.BlockSpec((lat_count, held, GROUP, wide), lambda g, t: (0, 0, g + start, 0)),
        ],
        out_specs=[pl.BlockSpec((1, half, wide), lambda g, t: (g * GROUP + t, 0, 0))] * lon_count,
        out_shape=[jax.ShapeDtypeStruct((count, half, wide), jnp.bfloat16)] * lon_count,
        scratch_shapes=[wide_scratch(lat_count * held * GROUP, wide)],
        compiler_params=pltpu.CompilerParams(vmem_limit_bytes=VMEM_LIMIT),
        cost_estimate=cost(0.8 * count),
    )(table, received)


def legendre_kernel(spectral_count, forward, table_ref, gain_ref, quad_ref, *refs):
    ins = refs[:spectral_count]
    refs = refs[spectral_count:]
    table = table_ref[0]
    rows = jnp.concatenate([ref[:, 0].astype(jnp.float32) for ref in ins], axis=1)
    lat_total, wide = rows.shape[0] * rows.shape[1], rows.shape[2]
    spectral = rows.reshape(lat_total, wide).astype(jnp.bfloat16)
    coefs = jnp.dot(table, spectral, preferred_element_type=jnp.float32)
    if forward:
        cot_ref, outs, sum_ref = refs[0], refs[1:-1], refs[-1]

        @pl.when(pl.program_id(0) == 0)
        def _():
            sum_ref[...] = jnp.zeros_like(sum_ref)

        sum_ref[...] += coefs * cot_ref[0]
    else:
        outs = refs[:-1]
        refs[-1][0] = coefs
    filtered = (gain_ref[...] * coefs).astype(jnp.bfloat16)
    synth = lax.dot_general(
        table, filtered, (((0,), (0,)), ((), ())), preferred_element_type=jnp.float32
    )
    if not forward:
        synth = synth * quad_ref[...]
    synth = synth.reshape(rows.shape)
    start = 0
    for ref in outs:
        count = ref.shape[2]
        ref[:, 0] = synth[:, start : start + count].astype(jnp.bfloat16)
        start += count


def legendre_call(table, gain, quad_all, received, spans, cot_coefs):
    lat_count, held, _, wide = received[0].shape
    degrees, lat_total = table.shape[1:]
    forward = cot_coefs is not None

    def chunk_spec(count):
        return pl.BlockSpec((lat_count, 1, count, wide), lambda i: (0, i, 0, 0))

    coef_spec = pl.BlockSpec((1, degrees, wide), lambda i: (i, 0, 0))
    in_specs = [
        pl.BlockSpec((1, degrees, lat_total), lambda i: (i, 0, 0)),
        pl.BlockSpec(gain.shape, lambda i: (0, 0)),
        pl.BlockSpec(quad_all.shape, lambda i: (0, 0)),
    ] + [chunk_spec(chunk.shape[2]) for chunk in received]
    operands = [table, gain, quad_all] + list(received)
    out_specs = [chunk_spec(count) for _, count in spans]
    out_shape = [
        jax.ShapeDtypeStruct((lat_count, held, count, wide), jnp.bfloat16) for _, count in spans
    ]
    if forward:
        in_specs.append(coef_spec)
        operands.append(cot_coefs)
        out_specs.append(pl.BlockSpec((degrees, wide), lambda i: (0, 0)))
        out_shape.append(jax.ShapeDtypeStruct((degrees, wide), jnp.float32))
    else:
        out_specs.append(coef_spec)
        out_shape.append(jax.ShapeDtypeStruct((held, degrees, wide), jnp.float32))
    outs = pl.pallas_call(
        functools.partial(legendre_kernel, len(received), forward),
        grid=(held,),
        in_specs=in_specs,
        out_specs=out_specs,
        out_shape=out_shape,
        compiler_params=pltpu.CompilerParams(vmem_limit_bytes=VMEM_LIMIT),
        cost_estimate=cost(1.1 * held),
    )(*operands)
    return outs[:-1], outs[-1]


def cot_conv_kernel(lon_count, place_ref, conv_ref, cot_ref, *refs):
    pieces, out_ref, scratch = refs[:lon_count], refs[-2], refs[-1]
    cot_hidden = unpack_row([ref[0] for ref in pieces], place_ref[0], scratch)
    slope = gelu_slope(conv_ref[0].astype(jnp.float32))
    out_ref[0] = (cot_ref[0].astype(jnp.float32) + cot_hidden * slope).astype(jnp.bfloat16)


def result_kernel(lon_count, place_ref, conv_ref, *refs):
    pieces, out_ref, scratch = refs[:lon_count], refs[-2], refs[-1]
    branch = unpack_row([ref[0] for ref in pieces], place_ref[0], scratch)
    out_ref[0] = (conv_ref[0].astype(jnp.float32) + branch).astype(jnp.bfloat16)


def grid_call(kernel, place, conv_out, beside, pieces, first, count, held):
    lon_count = len(pieces)
    cols, chans = conv_out.shape[1:]
    half, wide = pieces[0].shape[1:]
    row_spec = pl.BlockSpec((1, cols, chans), lambda t: (t + first, 0, 0))
    piece_spec = pl.BlockSpec((1, half, wide), lambda t: (t, 0, 0))
    in_specs = [SMEM_SPEC, row_spec] + [row_spec] * len(beside) + [piece_spec] * lon_count
    operands = [place, conv_out] + beside + list(pieces)
    aliases = {}
    if held is not None:
        aliases = {len(operands): 0}
        in_specs.append(pl.BlockSpec(memory_space=pl.ANY))
        operands.append(held)
    return pl.pallas_call(
        functools.partial(kernel, lon_count),
        grid=(count,),
        in_specs=in_specs,
        out_specs=row_spec,
        out_shape=jax.ShapeDtypeStruct(conv_out.shape, jnp.bfloat16),
        scratch_shapes=[pltpu.VMEM((lon_count, half, wide), jnp.float32)],
        input_output_aliases=aliases,
        compiler_params=pltpu.CompilerParams(vmem_limit_bytes=VMEM_LIMIT),
        cost_estimate=cost(0.9 * count),
    )(*operands)


def edges(block, axis, dim, width, periodic):
    count = lax.axis_size(axis)
    forward = [(i, i + 1) for i in range(count - 1)]
    if periodic:
        forward.append((count - 1, 0))
    backward = [(target, source) for source, target in forward]
    size = block.shape[dim]
    low = lax.ppermute(lax.slice_in_dim(block, size - width, size, axis=dim), axis, forward)
    high = lax.ppermute(lax.slice_in_dim(block, 0, width, axis=dim), axis, backward)
    return low, high


def padded_field(field, lat_edges, *gates):
    low, high = lat_edges
    cols = field.shape[1]
    ends = jnp.concatenate(
        [jnp.concatenate([part[:, :DW], part[:, cols - DW :]], axis=1) for part in (low, field, high)],
        axis=0,
    )
    west, east = edges(ends, "lon", 1, DW, True)
    tall = jnp.concatenate([low, after(field, *gates), high], axis=0)
    margin = jnp.zeros((tall.shape[0], Q_BLOCK - P_BLOCK - 2 * DW, tall.shape[2]), field.dtype)
    return jnp.concatenate([west, tall, east, margin], axis=1)


def after(value, *earlier):
    return lax.optimization_barrier((value,) + earlier)[0]


def swap(pieces, direction, earlier=None):
    count = lax.axis_size("lon")
    moved = [pieces[0]]
    for s in range(1, count):
        perm = [(i, (i + direction * s) % count) for i in range(count)]
        sent = pieces[s] if earlier is None else after(pieces[s], earlier)
        moved.append(lax.ppermute(sent, "lon", perm))
    return moved


def over_lat(blocks):
    return lax.all_to_all(blocks, "lat", split_axis=0, concat_axis=0, tiled=True)


def summed_everywhere(terms, gain_terms, gates, later_gate):
    lat_count, lon_count = lax.axis_size("lat"), lax.axis_size("lon")
    wide = terms.shape[1]
    parts = jnp.concatenate([terms, gain_terms], axis=1).astype(jnp.bfloat16)
    parts = parts.reshape(lat_count, -1, parts.shape[1])
    own = jnp.sum(over_lat(after(parts, *gates)).astype(jnp.float32), axis=0)
    pieces = jnp.stack(swap([own] * lon_count, 1))
    places = (lax.axis_index("lon") - jnp.arange(lon_count, dtype=jnp.int32)) % lon_count
    pieces = pieces[places]
    gains = [pieces[d, :, wide:] for d in range(lon_count)]
    total = jnp.concatenate([jnp.sum(pieces[:, :, :wide], axis=0)] + gains, axis=1).astype(jnp.bfloat16)
    shares = over_lat(after(jnp.broadcast_to(total[None], (lat_count,) + total.shape), later_gate))
    shares = shares.reshape(terms.shape[0], -1).astype(jnp.float32)
    return shares[:, :wide], shares[:, wide:]


def spans_of(*counts):
    spans, first = [], 0
    for count in counts:
        spans.append((first, count))
        first += count
    return spans


def body(
    source_field,
    cotangent,
    weight,
    spectral_gain,
    legendre,
    support_lat,
    support_lon,
    support_val,
    order_map,
):
    row_count, col_count, chan_count = source_field.shape
    lon_count, lat_count = lax.axis_size("lon"), lax.axis_size("lat")
    lat_total = row_count * lat_count
    band_index = lax.axis_index("lat")
    block_index = lax.axis_index("lon")
    share = chan_count // lon_count
    place = block_index.astype(jnp.int32).reshape(1)
    third = row_count // 3
    thirds = spans_of(third, third, row_count - 2 * third)
    spans = spans_of(row_count - third, third)

    back_places = (block_index - jnp.arange(lon_count, dtype=jnp.int32)) % lon_count
    longitude = (back_places[:, None] * col_count + jnp.arange(col_count, dtype=jnp.int32)).reshape(-1)
    orders = jnp.take(order_map.reshape(lat_count, lon_count, -1), back_places, axis=1).reshape(-1)
    inverse_table = dft_table(longitude, orders)
    forward_table = inverse_table.T
    all_rows = jnp.arange(lat_total, dtype=jnp.int32).astype(jnp.float32)
    quad_all = jnp.sin(math.pi * (all_rows + 0.5) / lat_total)
    quad_band = lax.dynamic_slice_in_dim(quad_all, band_index * row_count, row_count, 0)
    quad_rows = jnp.broadcast_to(quad_band[:, None, None], (row_count, 1, 2 * share))
    gain = lax.dynamic_slice_in_dim(spectral_gain, block_index * share, share, 1)
    gain = jnp.concatenate([gain, gain], axis=1)
    tap_weights = tap_table(support_lat, support_lon, support_val)
    tap_pad = jnp.pad(tap_weights, ((H, H), (0, 0), (0, 0), (0, 0)))
    tap_rows = lax.dynamic_slice_in_dim(tap_pad, band_index * row_count, row_count + 2 * H, 0)
    flat_weight = weight.reshape(K * chan_count, chan_count)
    flat_weight_back = weight.transpose(0, 2, 1).reshape(K * chan_count, chan_count)

    coefs = tap_coefficients(tap_rows, row_count, False)

    source_edges = edges(source_field, "lat", 0, H, False)
    packed = [pack_call(place, cotangent, lon_count, first, count) for first, count in thirds]
    padded_source, conv_out, hidden_pieces, last = None, None, [], None
    gates, cot_received, sent_gates = [pieces[0] for pieces in packed], [], source_edges
    for (first, count), pieces in zip(thirds, packed):
        lines = swap(pieces, 1, last)
        last = lines[-1]
        blocks = dft_call(
            forward_table, quad_rows, [[after(lines[0], *gates)] + lines[1:]], first, lat_count, False
        )
        cot_received.append(over_lat(after(blocks, *sent_gates)))
        sent_gates = [cot_received[-1]]
        if padded_source is None:
            padded_source = padded_field(source_field, source_edges, blocks)
        conv_out, pieces = conv_call(
            place, after(padded_source, blocks), coefs, flat_weight, col_count, lon_count, first, count, conv_out
        )
        gates = [conv_out]
        hidden_pieces.append(pieces)
    hidden_lines = []
    for pieces in hidden_pieces:
        hidden_lines.append(swap(pieces, 1, last))
        last = hidden_lines[-1][-1]
    table = jnp.concatenate(swap([legendre] * lon_count, 1, last), axis=0)
    hidden_blocks = dft_call(forward_table, quad_rows, hidden_lines, 0, lat_count, True)
    hidden_received = over_lat(after(hidden_blocks, cot_received[-1]))

    quad_column = quad_all[:, None]
    cot_synth, cot_coefs = legendre_call(
        after(table, hidden_blocks), gain, quad_column, cot_received, spans, None
    )
    synth, gain_terms = legendre_call(table, gain, quad_column, [hidden_received], spans, cot_coefs)
    first_back = over_lat(after(cot_synth[0], hidden_received))
    second_back = over_lat(after(cot_synth[1], first_back, synth[0]))
    cot_pieces = [swap(idft_call(inverse_table, after(first_back, synth[0]), lon_count, 0, third), -1)]
    last = cot_pieces[0][-1]
    first_branch = over_lat(after(synth[0], second_back, last))
    rest = row_count - 2 * third
    cot_pieces.append(
        swap(idft_call(inverse_table, after(first_back, last), lon_count, third, rest), -1, last)
    )
    last = cot_pieces[1][-1]
    cot_pieces.append(swap(idft_call(inverse_table, second_back, lon_count, 0, third), -1, last))
    cot_conv = None
    for (first, count), pieces in zip(spans_of(third, rest, third), cot_pieces):
        cot_conv = grid_call(
            cot_conv_kernel, place, conv_out, [cotangent], pieces, first, count, cot_conv
        )
    cot_edges = edges(cot_conv, "lat", 0, H, False)
    second_branch = over_lat(after(synth[1], first_branch, *cot_edges))
    padded_cot = padded_field(cot_conv, cot_edges)
    coefs_back = tap_coefficients(tap_rows, row_count, True)
    lines = idft_call(inverse_table, after(first_branch, padded_cot), lon_count, 0, row_count - third)
    first_lines = swap(lines, -1)
    padded_cot = after(padded_cot, lines[0])
    back = None
    for first, count in spans:
        back = back_call(padded_cot, coefs_back, flat_weight_back, source_field, first, count, back)
    grad_input, weight_part = back

    second_lines = idft_call(inverse_table, after(second_branch, grad_input), lon_count, 0, third)
    gates = [second_branch, first_lines[-1], second_lines[0]]
    second_lines = swap(second_lines, -1, first_lines[-1])
    result = None
    for (first, count), pieces in zip(spans, [first_lines, second_lines]):
        result = grid_call(result_kernel, place, conv_out, [], pieces, first, count, result)

    gain_part = gain_terms[:, :share] + gain_terms[:, share:]
    weight_total, gain_total = summed_everywhere(weight_part, gain_part, gates, second_lines[-1])
    weight_total = weight_total.reshape(chan_count, K, chan_count)
    grad_weight = weight_total.transpose(1, 0, 2) / math.sqrt(1.0 * lat_total * NLON)
    grad_gain = gain_total / math.sqrt(2.0 * M)
    return (result, grad_input, grad_weight, grad_gain)


def solution(mesh):
    return jax.shard_map(
        body,
        mesh=mesh,
        in_specs=(
            P("lat", "lon", None),
            P("lat", "lon", None),
            P(),
            P(),
            P(("lat", "lon"), None, None),
            P(),
            P(),
            P(),
            P(),
        ),
        out_specs=(P("lat", "lon", None), P("lat", "lon", None), P(), P()),
        check_vma=False,
    )
```

time: 1370 us -> 932 us (0.68)
  waiting for transfers between devices: 705 us -> 415 us
  Pallas kernels: 99 us -> 311 us
  local copies, waits for them, and re-layouts: 187 us -> 61 us
  matrix products: 127 us -> 3.9 us
  blocking collectives: 81.8 us -> 0 us
  other arithmetic: 61 us -> 40.4 us
    all_to_all x7 -> x10, waiting for transfers between devices: 565 us -> 185 us  [over_lat(): lax.all_to_all(blocks, 'lat', split_axis=0, concat_axis=0, tiled=True)]
    ppermute x8 -> x21, waiting for transfers between devices: 4.06 us -> 230 us  [the longest x13 199 us: swap(): moved.append(lax.ppermute(sent, 'lon', perm))]
    pallas_call x2 -> x24, Pallas kernels: 99 us -> 311 us  [the longest x2 59.7 us: back_call(): pl.pallas_call(functools.partial(back_kernel, held is not None), grid=(ro...]
    psum x1 -> x0, waiting for transfers between devices: 136 us -> none  [body(): lax.psum(weight_part, ('lat', 'lon')).reshape(chan_count, K, chan_count)]
    dot_general x8 -> x0, matrix products: 123 us -> none  [the longest x2 27.7 us: legendre_out(): jnp.einsum('olt,olqc->toqc', table_rows, coefficients, preferred_element_...]
    all_to_all x1 -> x0, blocking collectives: 81.8 us -> none  [to_grid(): lax.all_to_all(parts, 'lon', split_axis=0, concat_axis=0, tiled=True)]
    convert_element_type x2 -> x0, local copies, waits for them, and re-layouts: 47.9 us -> none  [body(): legendre_out(filtered, legendre).astype(jnp.bfloat16)]
    transpose x3 -> x1, local copies, waits for them, and re-layouts: 37.2 us -> 1.57 us  [body(): forward_table = inverse_table.T]
  transfers between devices with their start and end apart: 16 -> 31, of which waited for: 11 -> 20; matrix products, arithmetic and copies ran while one was open for 23% -> 7% of each run, Pallas kernels for 0% -> 34%
where the time goes in v1:
time: 932 us; the launch traced here: 922 us
  waiting for transfers between devices  415 us (45%)
  Pallas kernels  311 us (33%)
  starting transfers between devices  89.2 us (10%)
  local copies, waits for them, and re-layouts  61 us (7%)
  other arithmetic  40.4 us (4%)
    ppermute x13, waiting for transfers between devices, swap(): moved.append(lax.ppermute(sent, 'lon', perm))  199 us
    all_to_all x10, waiting for transfers between devices, over_lat(): lax.all_to_all(blocks, 'lat', split_axis=0, concat_axis=0, tiled=True)  185 us
    pallas_call x2, Pallas kernels, back_call(): pl.pallas_call(functools.partial(back_kernel, held is not None), grid=(ro...  59.7 us
    all_to_all x10, starting transfers between devices, over_lat(): lax.all_to_all(blocks, 'lat', split_axis=0, concat_axis=0, tiled=True)  59.1 us
    pallas_call x2, Pallas kernels, legendre_call(): pl.pallas_call(functools.partial(legendre_kernel, len(received), forward)...  54.6 us
    pallas_call x3, Pallas kernels, conv_call(): pl.pallas_call(functools.partial(conv_kernel, lon_count), grid=(row_count...  50.2 us
    pallas_call x5, Pallas kernels, idft_call(): pl.pallas_call(functools.partial(idft_kernel, lon_count), grid=(count //...  45.9 us
    pallas_call x5, Pallas kernels, grid_call(): pl.pallas_call(functools.partial(kernel, lon_count), grid=(count,), in_sp...  43.1 us
  transfers between devices with their start and end apart: 31, of which 20 were waited for; matrix products, arithmetic and copies ran while one was open for 7% of the time, Pallas kernels for 34%

profile of v1, /device:TPU:13, one launch (start us, length us, event | category | flops | bytes accessed | tf_op | source)
XLA Modules:
  0.0 921.7 jit_solution(12844153350574148928)
XLA Ops:
  44.5 8.6 shard_map.123
  75.2 11.9 %maximum_maximum_fusion.w0.w1.w2.w3.w4 = bf16[28,416,384]{2,1,0:T(8,128)(2,1)} fusion(bf16[28,4,384]{2,1,0:T(4,128)(2,1)} %collective-permute-done.4, bf16[2,384,384]{2,1,0:T(8,128)(2,1)} %copy-done.41, bf16[24,384,384]{2,1,0:T(8,128)(2,1)} %source_ref.3, bf16[2,384,384]{2,1,0:T(8,128)(2,1)S(1)} %copy-done.40, bf16[28,4,384]{2,1,0:T(4,128)(2,1)} %collective-permute-done.2, ...), kind=kLoop, calls=%fused_computation.2 | loop fusion | flops 53673984 | bytes 17376064 | tf_op jit(solution)/shard_map/concatenate | solution.py:509
  87.2 16.7 %shard_map.124 = (bf16[24,384,384]{2,1,0:T(8,128)(2,1)}, bf16[8,192,384]{2,1,0:T(8,128)(2,1)S(1)}, bf16[8,192,384]{2,1,0:T(8,128)(2,1)S(1)}) custom-call(s32[1]{0:T(128)} %bitcast.place_ref, f32[24,16,128]{2,1,0:T(8,128)S(1)} %pad.12.coef_ref, bf16[28,416,384]{2,1,0:T(8,128)(2,1)} %maximum_maximum_fusion.w0.w1.w2.w3.w4, ...), custom_call_target="tpu_custom_call" | custom-call | flops 5280000000 | bytes 16000000 | tf_op jit(solution)/shard_map/pallas_call | solution.py:218
  122.1 16.7 %shard_map.126 = (bf16[24,384,384]{2,1,0:T(8,128)(2,1)}, bf16[8,192,384]{2,1,0:T(8,128)(2,1)S(1)}, bf16[8,192,384]{2,1,0:T(8,128)(2,1)S(1)}) custom-call(s32[1]{0:T(128)} %bitcast.place_ref, f32[24,16,128]{2,1,0:T(8,128)S(1)} %pad.12.coef_ref, bf16[28,416,384]{2,1,0:T(8,128)(2,1)} %maximum_maximum_fusion.w0.w1.w2.w3.w4, ...), custom_call_target="tpu_custom_call", output_to_operand_aliasing={{0}: (8, {})} | custom-call | flops 5280000000 | bytes 16000000 | tf_op jit(solution)/shard_map/pallas_call | solution.py:218
  155.0 18.7 %all-to-all-done.1.refs_1_ = bf16[16,24,8,384]{3,2,1,0:T(8,128)(2,1)} async-done(((bf16[16,24,8,384]{3,2,1,0:T(8,128)(2,1)}), bf16[16,24,8,384]{3,2,1,0:T(8,128)(2,1)}, u32[]{:S(2)}, u32[]{:S(2)}) %all-to-all-start.1) | async-done | bytes 2359328 | tf_op jit(solution)/shard_map/all_to_all | solution.py:527
  179.9 26.1 %collective-permute-done.7.refs_1_ = bf16[8,192,384]{2,1,0:T(8,128)(2,1)S(1)} collective-permute-done((bf16[8,192,384]{2,1,0:T(8,128)(2,1)}, bf16[8,192,384]{2,1,0:T(8,128)(2,1)S(1)}, u32[]{:S(2)}, u32[]{:S(2)}) %collective-permute-start.7) | collective-permute-done | bytes 1179680 | tf_op jit(solution)/shard_map/ppermute | solution.py:522
  207.3 16.7 %shard_map.128 = (bf16[24,384,384]{2,1,0:T(8,128)(2,1)}, bf16[8,192,384]{2,1,0:T(8,128)(2,1)S(1)}, bf16[8,192,384]{2,1,0:T(8,128)(2,1)S(1)}) custom-call(s32[1]{0:T(128)} %bitcast.place_ref, f32[24,16,128]{2,1,0:T(8,128)S(1)} %pad.12.coef_ref, bf16[28,416,384]{2,1,0:T(8,128)(2,1)} %maximum_maximum_fusion.w0.w1.w2.w3.w4, ...), custom_call_target="tpu_custom_call", output_to_operand_aliasing={{0}: (8, {})} | custom-call | flops 5280000000 | bytes 16000000 | tf_op jit(solution)/shard_map/pallas_call | solution.py:218
  233.8 24.0 %collective-permute-done.9.refs_5_ = bf16[8,192,384]{2,1,0:T(8,128)(2,1)S(1)} collective-permute-done((bf16[8,192,384]{2,1,0:T(8,128)(2,1)S(1)}, bf16[8,192,384]{2,1,0:T(8,128)(2,1)S(1)}, u32[]{:S(2)}, u32[]{:S(2)}) %collective-permute-start.9) | collective-permute-done | bytes 1179680 | tf_op jit(solution)/shard_map/ppermute | solution.py:522
  258.9 22.0 %shard_map.129 = bf16[16,24,24,384]{3,2,1,0:T(8,128)(2,1)} custom-call(bf16[768,768]{1,0:T(8,128)(2,1)S(1)} %copy.104.table_ref, f32[24,1,384]{2,1,0:T(1,128)S(1)} %broadcast_in_dim.16.quad_ref, bf16[8,192,384]{2,1,0:T(8,128)(2,1)S(1)} %copy-done.26, bf16[8,192,384]{2,1,0:T(8,128)(2,1)S(1)} %collective-permute-done.7.refs_1_, ...), custom_call_target="tpu_custom_call" | custom-call | flops 7128000000 | bytes 21600000 | tf_op jit(solution)/shard_map/pallas_call | solution.py:309
  280.9 8.9 all-to-all-start.3
  294.5 73.3 %collective-permute-done.10 = bf16[12,384,384]{2,1,0:T(8,128)(2,1)} collective-permute-done((bf16[12,384,384]{2,1,0:T(8,128)(2,1)}, bf16[12,384,384]{2,1,0:T(8,128)(2,1)}, u32[]{:S(2)}, u32[]{:S(2)}) %collective-permute-start.10) | collective-permute-done | bytes 3538976 | tf_op jit(solution)/shard_map/ppermute | solution.py:522
  373.5 26.0 %shard_map.130 = (bf16[16,24,16,384]{3,2,1,0:T(8,128)(2,1)}, bf16[16,24,8,384]{3,2,1,0:T(8,128)(2,1)S(1)}, f32[24,384,384]{2,1,0:T(8,128)}) custom-call(bf16[24,384,384]{2,1,0:T(8,128)(2,1)} %copy-done.38, f32[384,384]{1,0:T(8,128)S(1)} %pad_maximum_fusion.1.gain_ref, f32[384,1]{1,0:T(8,128)S(1)} %sin.19.quad_ref, ...), custom_call_target="tpu_custom_call" | custom-call | flops 8711999488 | bytes 26400000 | tf_op jit(solution)/shard_map/pallas_call | solution.py:436
  401.0 43.1 %all-to-all-done.3.refs_0_ = bf16[16,24,24,384]{3,2,1,0:T(8,128)(2,1)} async-done(((bf16[16,24,24,384]{3,2,1,0:T(8,128)(2,1)}), bf16[16,24,24,384]{3,2,1,0:T(8,128)(2,1)}, u32[]{:S(2)}, u32[]{:S(2)}) %all-to-all-start.3) | async-done | bytes 7077920 | tf_op jit(solution)/shard_map/all_to_all | solution.py:527
  448.9 28.5 %shard_map.131 = (bf16[16,24,16,384]{3,2,1,0:T(8,128)(2,1)}, bf16[16,24,8,384]{3,2,1,0:T(8,128)(2,1)S(1)}, f32[384,384]{1,0:T(8,128)S(1)}) custom-call(bf16[24,384,384]{2,1,0:T(8,128)(2,1)} %copy-done.38, f32[384,384]{1,0:T(8,128)S(1)} %pad_maximum_fusion.1.gain_ref, f32[384,1]{1,0:T(8,128)S(1)} %sin.19.quad_ref, ...), custom_call_target="tpu_custom_call" | custom-call | flops 8711999488 | bytes 26400000 | tf_op jit(solution)/shard_map/pallas_call | solution.py:436
  479.7 73.0 %all-to-all-done.4.wide_in_ref = bf16[16,24,16,384]{3,2,1,0:T(8,128)(2,1)} async-done(((bf16[16,24,16,384]{3,2,1,0:T(8,128)(2,1)}), bf16[16,24,16,384]{3,2,1,0:T(8,128)(2,1)}, u32[]{:S(2)}, u32[]{:S(2)}) %all-to-all-start.4) | async-done | bytes 4718624 | tf_op jit(solution)/shard_map/all_to_all | solution.py:527
  559.2 7.8 shard_map.132
  568.3 26.1 %collective-permute-done.11.refs_1_ = bf16[8,192,384]{2,1,0:T(8,128)(2,1)S(1)} collective-permute-done((bf16[8,192,384]{2,1,0:T(8,128)(2,1)S(1)}, bf16[8,192,384]{2,1,0:T(8,128)(2,1)S(1)}, u32[]{:S(2)}, u32[]{:S(2)}) %collective-permute-start.11) | collective-permute-done | bytes 1179680 | tf_op jit(solution)/shard_map/ppermute | solution.py:522
  595.4 15.4 %all-to-all-done.5.wide_in_ref = bf16[16,24,8,384]{3,2,1,0:T(8,128)(2,1)} async-done(((bf16[16,24,8,384]{3,2,1,0:T(8,128)(2,1)}), bf16[16,24,8,384]{3,2,1,0:T(8,128)(2,1)}, u32[]{:S(2)}, u32[]{:S(2)}) %all-to-all-start.5) | async-done | bytes 2359328 | tf_op jit(solution)/shard_map/all_to_all | solution.py:527
  633.2 18.5 %collective-permute-done.12.refs_1_ = bf16[8,192,384]{2,1,0:T(8,128)(2,1)S(1)} collective-permute-done((bf16[8,192,384]{2,1,0:T(8,128)(2,1)S(1)}, bf16[8,192,384]{2,1,0:T(8,128)(2,1)S(1)}, u32[]{:S(2)}, u32[]{:S(2)}) %collective-permute-start.12) | collective-permute-done | bytes 1179680 | tf_op jit(solution)/shard_map/ppermute | solution.py:522
  653.0 7.7 shard_map.135.refs_2_
  660.7 7.7 shard_map.136.refs_2_
  668.4 9.7 %collective-permute-done.13.refs_1_ = bf16[8,192,384]{2,1,0:T(8,128)(2,1)S(1)} collective-permute-done((bf16[8,192,384]{2,1,0:T(8,128)(2,1)S(1)}, bf16[8,192,384]{2,1,0:T(8,128)(2,1)S(1)}, u32[]{:S(2)}, u32[]{:S(2)}) %collective-permute-start.13) | collective-permute-done | bytes 1179680 | tf_op jit(solution)/shard_map/ppermute | solution.py:522
  678.1 7.7 shard_map.137
  698.3 27.4 %collective-permute-done.15 = bf16[2,384,384]{2,1,0:T(8,128)(2,1)S(1)} collective-permute-done((bf16[2,384,384]{2,1,0:T(8,128)(2,1)}, bf16[2,384,384]{2,1,0:T(8,128)(2,1)S(1)}, u32[]{:S(2)}, u32[]{:S(2)}) %collective-permute-start.15) | collective-permute-done | bytes 589856 | tf_op jit(solution)/shard_map/ppermute | solution.py:495
  736.6 16.0 %maximum_maximum_fusion.1.w0.w1.w2.w3.w4 = bf16[28,416,384]{2,1,0:T(8,128)(2,1)} fusion(bf16[28,4,384]{2,1,0:T(4,128)(2,1)} %collective-permute-done.17, bf16[2,384,384]{2,1,0:T(8,128)(2,1)S(1)} %copy-done.43, bf16[24,384,384]{2,1,0:T(8,128)(2,1)} %shard_map.137, bf16[2,384,384]{2,1,0:T(8,128)(2,1)} %copy-done.44, ...), kind=kLoop, calls=%fused_computation.3 | loop fusion | flops 53673984 | bytes 17376064 | tf_op jit(solution)/shard_map/concatenate | solution.py:509
  752.5 15.2 %shard_map.138 = (bf16[16,192,384]{2,1,0:T(8,128)(2,1)S(1)}, bf16[16,192,384]{2,1,0:T(8,128)(2,1)}) custom-call(bf16[768,768]{1,0:T(8,128)(2,1)S(1)} %copy-done.16, bf16[16,24,16,384]{3,2,1,0:T(8,128)(2,1)} %all-to-all-done.6.wide_in_ref), custom_call_target="tpu_custom_call" | custom-call | flops 4224000000 | bytes 12800000 | tf_op jit(solution)/shard_map/pallas_call | solution.py:361
  770.6 39.2 %shard_map.139 = (bf16[24,384,384]{2,1,0:T(8,128)(2,1)}, f32[384,1152]{1,0:T(8,128)S(1)}) custom-call(f32[24,16,128]{2,1,0:T(8,128)S(1)} %pad.13.coef_ref, bf16[28,416,384]{2,1,0:T(8,128)(2,1)} %maximum_maximum_fusion.1.w0.w1.w2.w3.w4, bf16[28,416,384]{2,1,0:T(8,128)(2,1)} %maximum_maximum_fusion.1.w0.w1.w2.w3.w4, ...), custom_call_target="tpu_custom_call" | custom-call | flops 12672000000 | bytes 38400000 | tf_op jit(solution)/shard_map/pallas_call | solution.py:247
  809.8 20.5 %shard_map.140 = (bf16[24,384,384]{2,1,0:T(8,128)(2,1)}, f32[384,1152]{1,0:T(8,128)S(1)}) custom-call(f32[24,16,128]{2,1,0:T(8,128)S(1)} %pad.13.coef_ref, bf16[28,416,384]{2,1,0:T(8,128)(2,1)} %maximum_maximum_fusion.1.w0.w1.w2.w3.w4, bf16[28,416,384]{2,1,0:T(8,128)(2,1)} %maximum_maximum_fusion.1.w0.w1.w2.w3.w4, ...), custom_call_target="tpu_custom_call", output_to_operand_aliasing={{0}: (8, {})} | custom-call | flops 6336000000 | bytes 19200000 | tf_op jit(solution)/shard_map/pallas_call | solution.py:247
  831.5 8.1 shard_map.141
  847.6 25.8 %all-to-all-done.8 = bf16[16,24,1344]{2,1,0:T(8,128)(2,1)S(1)} async-done(((bf16[16,24,1344]{2,1,0:T(8,128)(2,1)}), bf16[16,24,1344]{2,1,0:T(8,128)(2,1)S(1)}, u32[]{:S(2)}, u32[]{:S(2)}) %all-to-all-start.8) | async-done | bytes 1032224 | tf_op jit(solution)/shard_map/all_to_all | solution.py:527
  886.5 13.0 %shard_map.142.refs_2_ = bf16[24,384,384]{2,1,0:T(8,128)(2,1)} custom-call(s32[1]{0:T(128)} %bitcast.place_ref, bf16[24,384,384]{2,1,0:T(8,128)(2,1)} %get-tuple-element.88.conv_ref, bf16[16,192,384]{2,1,0:T(8,128)(2,1)S(1)} %copy-done.8, bf16[16,192,384]{2,1,0:T(8,128)(2,1)} %collective-permute-done.18.refs_1_), custom_call_target="tpu_custom_call" | custom-call | flops 4752000000 | bytes 14400000 | tf_op jit(solution)/shard_map/pallas_call | solution.py:474
  906.5 7.8 all-to-all-done.9
  (234 shorter events, 232.1 us)
Async XLA Ops:
  0.6 291.2 %copy-start = (f32[384,384]{1,0:T(8,128)S(1)}, f32[384,384]{1,0:T(8,128)}, u32[]{:S(2)}) copy-start(f32[384,384]{1,0:T(8,128)} %param.12) | copy-start | bytes 1769476
  3.1 50.1 %collective-permute-start = (bf16[2,384,384]{2,1,0:T(8,128)(2,1)}, bf16[2,384,384]{2,1,0:T(8,128)(2,1)S(1)}, u32[]{:S(2)}, u32[]{:S(2)}) collective-permute-start(bf16[2,384,384]{2,1,0:T(8,128)(2,1)} %get-tuple-element.162), channel_id=1, source_target_pairs={{0,2},{2,4},{4,6},{6,8},{8,10},{10,12},{12,14},{14,16},{16,18},{18... | collective-permute-start | bytes 1769480 | tf_op jit(solution)/shard_map/ppermute | solution.py:494
  6.8 46.4 %collective-permute-start.1 = (bf16[2,384,384]{2,1,0:T(8,128)(2,1)}, bf16[2,384,384]{2,1,0:T(8,128)(2,1)S(1)}, u32[]{:S(2)}, u32[]{:S(2)}) collective-permute-start(bf16[2,384,384]{2,1,0:T(8,128)(2,1)} %get-tuple-element.163), channel_id=1, source_target_pairs={{2,0},{4,2},{6,4},{8,6},{10,8},{12,10},{14,12},{16,14},{18,16},{20... | collective-permute-start | bytes 1769480 | tf_op jit(solution)/shard_map/ppermute | solution.py:495
  15.9 27.2 %collective-permute-start.3 = (bf16[8,192,384]{2,1,0:T(8,128)(2,1)}, bf16[8,192,384]{2,1,0:T(8,128)(2,1)}, u32[]{:S(2)}, u32[]{:S(2)}) collective-permute-start(bf16[8,192,384]{2,1,0:T(8,128)(2,1)} %get-tuple-element.75), channel_id=1, source_target_pairs={{0,1},{1,0},{2,3},{3,2},{4,5},{5,4},{6,7},{7,6},{8,9},{9,8},{10,11... | collective-permute-start | bytes 3538952 | tf_op jit(solution)/shard_map/ppermute | solution.py:522
  54.2 59.8 %all-to-all-start = ((bf16[16,24,8,384]{3,2,1,0:T(8,128)(2,1)}), bf16[16,24,8,384]{3,2,1,0:T(8,128)(2,1)}, u32[]{:S(2)}, u32[]{:S(2)}) async-start(bf16[16,24,8,384]{3,2,1,0:T(8,128)(2,1)} %shard_map.123), calls=%async_computation | async-start | bytes 4718592 | tf_op jit(solution)/shard_map/all_to_all | solution.py:527
  69.2 4.1 collective-permute-start.2
  70.4 4.9 collective-permute-start.4
  70.8 35.1 %collective-permute-start.5 = (bf16[8,192,384]{2,1,0:T(8,128)(2,1)}, bf16[8,192,384]{2,1,0:T(8,128)(2,1)S(1)}, u32[]{:S(2)}, u32[]{:S(2)}) collective-permute-start(bf16[8,192,384]{2,1,0:T(8,128)(2,1)} %copy-done.24), channel_id=1, source_target_pairs={{0,1},{1,0},{2,3},{3,2},{4,5},{5,4},{6,7},{7,6},{8,9},{9,8},{10,11... | collective-permute-start | bytes 3538952 | tf_op jit(solution)/shard_map/ppermute | solution.py:522
  113.9 59.8 %all-to-all-start.1 = ((bf16[16,24,8,384]{3,2,1,0:T(8,128)(2,1)}), bf16[16,24,8,384]{3,2,1,0:T(8,128)(2,1)}, u32[]{:S(2)}, u32[]{:S(2)}) async-start(bf16[16,24,8,384]{3,2,1,0:T(8,128)(2,1)} %copy-done.6), calls=%async_computation.1 | async-start | bytes 4718592 | tf_op jit(solution)/shard_map/all_to_all | solution.py:527
  120.7 27.5 %collective-permute-start.6 = (bf16[8,192,384]{2,1,0:T(8,128)(2,1)}, bf16[8,192,384]{2,1,0:T(8,128)(2,1)S(1)}, u32[]{:S(2)}, u32[]{:S(2)}) collective-permute-start(bf16[8,192,384]{2,1,0:T(8,128)(2,1)} %copy-done.21), channel_id=1, source_target_pairs={{0,1},{1,0},{2,3},{3,2},{4,5},{5,4},{6,7},{7,6},{8,9},{9,8},{10,11... | collective-permute-start | bytes 3538952 | tf_op jit(solution)/shard_map/ppermute | solution.py:522
  173.7 107.2 %all-to-all-start.2 = ((bf16[16,24,8,384]{3,2,1,0:T(8,128)(2,1)}), bf16[16,24,8,384]{3,2,1,0:T(8,128)(2,1)}, u32[]{:S(2)}, u32[]{:S(2)}) async-start(bf16[16,24,8,384]{3,2,1,0:T(8,128)(2,1)} %copy-done.4), calls=%async_computation.2 | async-start | bytes 4718592 | tf_op jit(solution)/shard_map/all_to_all | solution.py:527
  178.6 27.4 %collective-permute-start.7 = (bf16[8,192,384]{2,1,0:T(8,128)(2,1)}, bf16[8,192,384]{2,1,0:T(8,128)(2,1)S(1)}, u32[]{:S(2)}, u32[]{:S(2)}) collective-permute-start(bf16[8,192,384]{2,1,0:T(8,128)(2,1)} %copy-done.31), channel_id=1, source_target_pairs={{0,1},{1,0},{2,3},{3,2},{4,5},{5,4},{6,7},{7,6},{8,9},{9,8},{10,11... | collective-permute-start | bytes 3538952 | tf_op jit(solution)/shard_map/ppermute | solution.py:522
  206.0 26.5 %collective-permute-start.8 = (bf16[8,192,384]{2,1,0:T(8,128)(2,1)}, bf16[8,192,384]{2,1,0:T(8,128)(2,1)S(1)}, u32[]{:S(2)}, u32[]{:S(2)}) collective-permute-start(bf16[8,192,384]{2,1,0:T(8,128)(2,1)} %copy-done.32), channel_id=1, source_target_pairs={{0,1},{1,0},{2,3},{3,2},{4,5},{5,4},{6,7},{7,6},{8,9},{9,8},{10,11... | collective-permute-start | bytes 3538952 | tf_op jit(solution)/shard_map/ppermute | solution.py:522
  232.5 25.3 %collective-permute-start.9 = (bf16[8,192,384]{2,1,0:T(8,128)(2,1)S(1)}, bf16[8,192,384]{2,1,0:T(8,128)(2,1)S(1)}, u32[]{:S(2)}, u32[]{:S(2)}) collective-permute-start(bf16[8,192,384]{2,1,0:T(8,128)(2,1)S(1)} %get-tuple-element.94), channel_id=1, source_target_pairs={{0,1},{1,0},{2,3},{3,2},{4,5},{5,4},{6,7},{7,6},{8,9},{9,8},{10,11... | collective-permute-start | bytes 3538952 | tf_op jit(solution)/shard_map/ppermute | solution.py:522
  280.9 163.2 %all-to-all-start.3 = ((bf16[16,24,24,384]{3,2,1,0:T(8,128)(2,1)}), bf16[16,24,24,384]{3,2,1,0:T(8,128)(2,1)}, u32[]{:S(2)}, u32[]{:S(2)}) async-start(bf16[16,24,24,384]{3,2,1,0:T(8,128)(2,1)} %shard_map.129), calls=%async_computation.3 | async-start | bytes 14155776 | tf_op jit(solution)/shard_map/all_to_all | solution.py:527
  289.8 78.1 %collective-permute-start.10 = (bf16[12,384,384]{2,1,0:T(8,128)(2,1)}, bf16[12,384,384]{2,1,0:T(8,128)(2,1)}, u32[]{:S(2)}, u32[]{:S(2)}) collective-permute-start(bf16[12,384,384]{2,1,0:T(8,128)(2,1)} %param.13), channel_id=1, source_target_pairs={{0,1},{1,0},{2,3},{3,2},{4,5},{5,4},{6,7},{7,6},{8,9},{9,8},{10,11... | collective-permute-start | bytes 10616840 | tf_op jit(solution)/shard_map/ppermute | solution.py:522
  444.0 108.6 %all-to-all-start.4 = ((bf16[16,24,16,384]{3,2,1,0:T(8,128)(2,1)}), bf16[16,24,16,384]{3,2,1,0:T(8,128)(2,1)}, u32[]{:S(2)}, u32[]{:S(2)}) async-start(bf16[16,24,16,384]{3,2,1,0:T(8,128)(2,1)} %get-tuple-element.109), calls=%async_computation.4 | async-start | bytes 9437184 | tf_op jit(solution)/shard_map/all_to_all | solution.py:527
  552.6 58.2 %all-to-all-start.5 = ((bf16[16,24,8,384]{3,2,1,0:T(8,128)(2,1)}), bf16[16,24,8,384]{3,2,1,0:T(8,128)(2,1)}, u32[]{:S(2)}, u32[]{:S(2)}) async-start(bf16[16,24,8,384]{3,2,1,0:T(8,128)(2,1)} %copy-done.5), calls=%async_computation.5 | async-start | bytes 4718592 | tf_op jit(solution)/shard_map/all_to_all | solution.py:527
  567.0 27.4 %collective-permute-start.11 = (bf16[8,192,384]{2,1,0:T(8,128)(2,1)S(1)}, bf16[8,192,384]{2,1,0:T(8,128)(2,1)S(1)}, u32[]{:S(2)}, u32[]{:S(2)}) collective-permute-start(bf16[8,192,384]{2,1,0:T(8,128)(2,1)S(1)} %get-tuple-element.112), channel_id=1, source_target_pairs={{0,1},{1,0},{2,3},{3,2},{4,5},{5,4},{6,7},{7,6},{8,9},{9,8},{10,11... | collective-permute-start | bytes 3538952 | tf_op jit(solution)/shard_map/ppermute | solution.py:522
  610.8 118.0 %all-to-all-start.6 = ((bf16[16,24,16,384]{3,2,1,0:T(8,128)(2,1)}), bf16[16,24,16,384]{3,2,1,0:T(8,128)(2,1)}, u32[]{:S(2)}, u32[]{:S(2)}) async-start(bf16[16,24,16,384]{3,2,1,0:T(8,128)(2,1)} %get-tuple-element.113), calls=%async_computation.6 | async-start | bytes 9437184 | tf_op jit(solution)/shard_map/all_to_all | solution.py:527
  624.5 27.3 %collective-permute-start.12 = (bf16[8,192,384]{2,1,0:T(8,128)(2,1)S(1)}, bf16[8,192,384]{2,1,0:T(8,128)(2,1)S(1)}, u32[]{:S(2)}, u32[]{:S(2)}) collective-permute-start(bf16[8,192,384]{2,1,0:T(8,128)(2,1)S(1)} %get-tuple-element.118), channel_id=1, source_target_pairs={{0,1},{1,0},{2,3},{3,2},{4,5},{5,4},{6,7},{7,6},{8,9},{9,8},{10,11... | collective-permute-start | bytes 3538952 | tf_op jit(solution)/shard_map/ppermute | solution.py:522
  651.7 26.4 %collective-permute-start.13 = (bf16[8,192,384]{2,1,0:T(8,128)(2,1)S(1)}, bf16[8,192,384]{2,1,0:T(8,128)(2,1)S(1)}, u32[]{:S(2)}, u32[]{:S(2)}) collective-permute-start(bf16[8,192,384]{2,1,0:T(8,128)(2,1)S(1)} %get-tuple-element.119), channel_id=1, source_target_pairs={{0,1},{1,0},{2,3},{3,2},{4,5},{5,4},{6,7},{7,6},{8,9},{9,8},{10,11... | collective-permute-start | bytes 3538952 | tf_op jit(solution)/shard_map/ppermute | solution.py:522
  688.0 37.7 %collective-permute-start.15 = (bf16[2,384,384]{2,1,0:T(8,128)(2,1)}, bf16[2,384,384]{2,1,0:T(8,128)(2,1)S(1)}, u32[]{:S(2)}, u32[]{:S(2)}) collective-permute-start(bf16[2,384,384]{2,1,0:T(8,128)(2,1)} %get-tuple-element.160), channel_id=1, source_target_pairs={{2,0},{4,2},{6,4},{8,6},{10,8},{12,10},{14,12},{16,14},{18,16},{20... | collective-permute-start | bytes 1769480 | tf_op jit(solution)/shard_map/ppermute | solution.py:495
  691.9 33.8 %collective-permute-start.14 = (bf16[2,384,384]{2,1,0:T(8,128)(2,1)S(1)}, bf16[2,384,384]{2,1,0:T(8,128)(2,1)S(1)}, u32[]{:S(2)}, u32[]{:S(2)}) collective-permute-start(bf16[2,384,384]{2,1,0:T(8,128)(2,1)S(1)} %get-tuple-element.161), channel_id=1, source_target_pairs={{0,2},{2,4},{4,6},{6,8},{8,10},{10,12},{12,14},{14,16},{16,18},{18... | collective-permute-start | bytes 1769480 | tf_op jit(solution)/shard_map/ppermute | solution.py:494
  727.4 9.2 collective-permute-start.16
  728.6 7.9 collective-permute-start.17
  728.8 102.6 %all-to-all-start.7 = ((bf16[16,24,8,384]{3,2,1,0:T(8,128)(2,1)}), bf16[16,24,8,384]{3,2,1,0:T(8,128)(2,1)}, u32[]{:S(2)}, u32[]{:S(2)}) async-start(bf16[16,24,8,384]{3,2,1,0:T(8,128)(2,1)} %copy-done.3), calls=%async_computation.7 | async-start | bytes 4718592 | tf_op jit(solution)/shard_map/all_to_all | solution.py:527
  769.2 71.4 %collective-permute-start.18 = (bf16[16,192,384]{2,1,0:T(8,128)(2,1)}, bf16[16,192,384]{2,1,0:T(8,128)(2,1)}, u32[]{:S(2)}, u32[]{:S(2)}) collective-permute-start(bf16[16,192,384]{2,1,0:T(8,128)(2,1)} %get-tuple-element.132), channel_id=1, source_target_pairs={{0,1},{1,0},{2,3},{3,2},{4,5},{5,4},{6,7},{7,6},{8,9},{9,8},{10,11... | collective-permute-start | bytes 7077896 | tf_op jit(solution)/shard_map/ppermute | solution.py:522
  840.6 32.8 %all-to-all-start.8 = ((bf16[16,24,1344]{2,1,0:T(8,128)(2,1)}), bf16[16,24,1344]{2,1,0:T(8,128)(2,1)S(1)}, u32[]{:S(2)}, u32[]{:S(2)}) async-start(bf16[16,24,1344]{2,1,0:T(8,128)(2,1)} %pad_maximum_fusion), calls=%async_computation.8 | async-start | bytes 2162688 | tf_op jit(solution)/shard_map/all_to_all | solution.py:527
  847.4 32.5 %collective-permute-start.19 = (bf16[8,192,384]{2,1,0:T(8,128)(2,1)}, bf16[8,192,384]{2,1,0:T(8,128)(2,1)}, u32[]{:S(2)}, u32[]{:S(2)}) collective-permute-start(bf16[8,192,384]{2,1,0:T(8,128)(2,1)} %get-tuple-element.133), channel_id=1, source_target_pairs={{0,1},{1,0},{2,3},{3,2},{4,5},{5,4},{6,7},{7,6},{8,9},{9,8},{10,11... | collective-permute-start | bytes 3538952 | tf_op jit(solution)/shard_map/ppermute | solution.py:522
  873.6 5.4 collective-permute-start.20
  880.9 33.4 %all-to-all-start.9 = ((bf16[16,24,1536]{2,1,0:T(8,128)(2,1)}), bf16[16,24,1536]{2,1,0:T(8,128)(2,1)}, u32[]{:S(2)}, u32[]{:S(2)}) async-start(bf16[16,24,1536]{2,1,0:T(8,128)(2,1)} %broadcast_in_dim.17), calls=%async_computation.9 | async-start | bytes 2359296 | tf_op jit(solution)/shard_map/all_to_all | solution.py:527
  (50 other events, 364.6 us)

commit v2 on v1

--- a/solution.py
+++ b/solution.py
@@ -52,6 +52,7 @@
 VMEM_LIMIT = 48 * 1024 * 1024
 GROUP = 8
 LANES = 128
+WEST = 8
 
 
 def lane_tiles(wide):
@@ -64,7 +65,7 @@
 
 def cost(micros):
     return pl.CostEstimate(
-        flops=int(micros * 3.3e8), bytes_accessed=int(micros * 1e6), transcendentals=0
+        flops=int(micros * 6e8), bytes_accessed=int(micros * 2e6), transcendentals=0
     )
 
 
@@ -77,7 +78,7 @@
             taken = tap_rows[H : H + row_count, :, place, :]
         coef_list.append(taken)
     coefs = jnp.stack(coef_list, axis=2).reshape(row_count, K * N_LAT_TAPS, 2 * DW + 1)
-    return jnp.pad(coefs, ((0, 0), (0, 1), (0, Q_BLOCK - 2 * DW - 1)))
+    return jnp.pad(coefs, ((0, 0), (0, 1), (WEST - DW, Q_BLOCK - WEST - DW - 1)))
 
 
 def fill_taps(coef_ref, window_refs, band_ref, taps_ref):
@@ -505,8 +506,9 @@
     )
     west, east = edges(ends, "lon", 1, DW, True)
     tall = jnp.concatenate([low, after(field, *gates), high], axis=0)
-    margin = jnp.zeros((tall.shape[0], Q_BLOCK - P_BLOCK - 2 * DW, tall.shape[2]), field.dtype)
-    return jnp.concatenate([west, tall, east, margin], axis=1)
+    west = jnp.pad(west, ((0, 0), (WEST - DW, 0), (0, 0)))
+    east = jnp.pad(east, ((0, 0), (0, Q_BLOCK - P_BLOCK - WEST - DW), (0, 0)))
+    return jnp.concatenate([west, tall, east], axis=1)
 
 
 def after(value, *earlier):
@@ -616,44 +618,50 @@
         hidden_lines.append(swap(pieces, 1, last))
         last = hidden_lines[-1][-1]
     table = jnp.concatenate(swap([legendre] * lon_count, 1, last), axis=0)
-    hidden_blocks = dft_call(forward_table, quad_rows, hidden_lines, 0, lat_count, True)
-    hidden_received = over_lat(after(hidden_blocks, cot_received[-1]))
+    hidden_received = []
+    sent_gates.append(hidden_lines[1][-1])
+    for first, lines in ((0, hidden_lines[:1]), (third, hidden_lines[1:])):
+        if first == 0:
+            lines = [[after(lines[0][0], conv_out)] + lines[0][1:]]
+        blocks = dft_call(forward_table, quad_rows, lines, first, lat_count, True)
+        hidden_received.append(over_lat(after(blocks, *sent_gates)))
+        sent_gates = [hidden_received[-1]]
 
     quad_column = quad_all[:, None]
     cot_synth, cot_coefs = legendre_call(
-        after(table, hidden_blocks), gain, quad_column, cot_received, spans, None
-    )
-    synth, gain_terms = legendre_call(table, gain, quad_column, [hidden_received], spans, cot_coefs)
-    first_back = over_lat(after(cot_synth[0], hidden_received))
-    second_back = over_lat(after(cot_synth[1], first_back, synth[0]))
-    cot_pieces = [swap(idft_call(inverse_table, after(first_back, synth[0]), lon_count, 0, third), -1)]
-    last = cot_pieces[0][-1]
-    first_branch = over_lat(after(synth[0], second_back, last))
-    rest = row_count - 2 * third
-    cot_pieces.append(
-        swap(idft_call(inverse_table, after(first_back, last), lon_count, third, rest), -1, last)
-    )
-    last = cot_pieces[1][-1]
-    cot_pieces.append(swap(idft_call(inverse_table, second_back, lon_count, 0, third), -1, last))
-    cot_conv = None
-    for (first, count), pieces in zip(spans_of(third, rest, third), cot_pieces):
+        after(table, blocks), gain, quad_column, cot_received, thirds, None
+    )
+    outer_first = [0, 2, 1]
+    first_back = over_lat(after(cot_synth[0], *sent_gates))
+    synth, gain_terms = legendre_call(table, gain, quad_column, hidden_received, spans, cot_coefs)
+
+    cot_conv, received, gates = None, first_back, [synth[0]]
+    for step, index in enumerate(outer_first):
+        first, count = thirds[index]
+        later = synth[0] if step == 2 else cot_synth[outer_first[step + 1]]
+        later = over_lat(after(later, received, *gates))
+        pieces = idft_call(inverse_table, after(received, gates[0]), lon_count, 0, count)
+        pieces = swap(pieces, -1, None if cot_conv is None else gates[0])
         cot_conv = grid_call(
             cot_conv_kernel, place, conv_out, [cotangent], pieces, first, count, cot_conv
         )
-    cot_edges = edges(cot_conv, "lat", 0, H, False)
-    second_branch = over_lat(after(synth[1], first_branch, *cot_edges))
+        received, gates = later, [pieces[-1]]
+        if step == 1:
+            cot_edges = edges(cot_conv, "lat", 0, H, False)
+            gates += list(cot_edges)
+    first_branch = received
     padded_cot = padded_field(cot_conv, cot_edges)
     coefs_back = tap_coefficients(tap_rows, row_count, True)
-    lines = idft_call(inverse_table, after(first_branch, padded_cot), lon_count, 0, row_count - third)
+    (first, count), (last_first, last_count) = spans
+    back = back_call(padded_cot, coefs_back, flat_weight_back, source_field, first, count, None)
+    second_branch = over_lat(after(synth[1], first_branch, back[0]))
+    lines = idft_call(inverse_table, after(first_branch, back[0]), lon_count, 0, count)
+    grad_input, weight_part = back_call(
+        after(padded_cot, lines[0]), coefs_back, flat_weight_back, source_field, last_first, last_count, back
+    )
     first_lines = swap(lines, -1)
-    padded_cot = after(padded_cot, lines[0])
-    back = None
-    for first, count in spans:
-        back = back_call(padded_cot, coefs_back, flat_weight_back, source_field, first, count, back)
-    grad_input, weight_part = back
-
-    second_lines = idft_call(inverse_table, after(second_branch, grad_input), lon_count, 0, third)
-    gates = [second_branch, first_lines[-1], second_lines[0]]
+    second_lines = idft_call(inverse_table, after(second_branch, grad_input), lon_count, 0, spans[1][1])
+    gates = [second_branch]
     second_lines = swap(second_lines, -1, first_lines[-1])
     result = None
     for (first, count), pieces in zip(spans, [first_lines, second_lines]):

time: 932 us -> 876 us (0.940)
  waiting for transfers between devices: 415 us -> 341 us
  starting transfers between devices: 89.2 us -> 100 us
    all_to_all x10 -> x12, waiting for transfers between devices: 185 us -> 105 us  [over_lat(): lax.all_to_all(blocks, 'lat', split_axis=0, concat_axis=0, tiled=True)]
    ppermute x13, waiting for transfers between devices: 199 us -> 224 us  [swap(): moved.append(lax.ppermute(sent, 'lon', perm))]
    all_to_all x10 -> x12, starting transfers between devices: 59.1 us -> 79 us  [over_lat(): lax.all_to_all(blocks, 'lat', split_axis=0, concat_axis=0, tiled=True)]
    ppermute x4, waiting for transfers between devices: 29.4 us -> 10.5 us  [edges(): lax.ppermute(lax.slice_in_dim(block, 0, width, axis=dim), axis, backward)]
    unnamed x107 -> x111, local copies, waits for them, and re-layouts: 35.8 us -> 43.2 us
    pallas_call x4 -> x5, Pallas kernels: 41.4 us -> 38.3 us  [dft_call(): pl.pallas_call(functools.partial(dft_kernel, scaled, lon_count, starts),...]
  transfers between devices with their start and end apart: 31 -> 33, of which waited for: 20 -> 23; matrix products, arithmetic and copies ran while one was open for 7% -> 7% of each run, Pallas kernels for 34% -> 36%
where the time goes in v2:
time: 876 us; the launch traced here: 865 us
  waiting for transfers between devices  341 us (39%)
  Pallas kernels  309 us (35%)
  starting transfers between devices  100 us (11%)
  local copies, waits for them, and re-layouts  66.5 us (8%)
  other arithmetic  41.1 us (5%)
    ppermute x13, waiting for transfers between devices, swap(): moved.append(lax.ppermute(sent, 'lon', perm))  224 us
    all_to_all x12, waiting for transfers between devices, over_lat(): lax.all_to_all(blocks, 'lat', split_axis=0, concat_axis=0, tiled=True)  105 us
    all_to_all x12, starting transfers between devices, over_lat(): lax.all_to_all(blocks, 'lat', split_axis=0, concat_axis=0, tiled=True)  79 us
    pallas_call x2, Pallas kernels, back_call(): pl.pallas_call(functools.partial(back_kernel, held is not None), grid=(ro...  59.7 us
    pallas_call x2, Pallas kernels, legendre_call(): pl.pallas_call(functools.partial(legendre_kernel, len(received), forward)...  54.6 us
    pallas_call x3, Pallas kernels, conv_call(): pl.pallas_call(functools.partial(conv_kernel, lon_count), grid=(row_count...  50.2 us
    pallas_call x5, Pallas kernels, idft_call(): pl.pallas_call(functools.partial(idft_kernel, lon_count), grid=(count //...  46.7 us
    pallas_call x5, Pallas kernels, grid_call(): pl.pallas_call(functools.partial(kernel, lon_count), grid=(count,), in_sp...  43.3 us
  transfers between devices with their start and end apart: 33, of which 23 were waited for; matrix products, arithmetic and copies ran while one was open for 7% of the time, Pallas kernels for 36%

profile of v2, /device:TPU:13, one launch (start us, length us, event | category | flops | bytes accessed | tf_op | source)
XLA Modules:
  0.0 864.9 jit_solution(12131492194831937035)
XLA Ops:
  48.4 8.6 shard_map.123
  71.7 13.8 %fusion.5.w0.w1.w2.w3.w4 = bf16[28,416,384]{2,1,0:T(8,128)(2,1)} fusion(bf16[28,4,384]{2,1,0:T(4,128)(2,1)S(1)} %collective-permute-done.4, bf16[28,4,384]{2,1,0:T(4,128)(2,1)S(1)} %collective-permute-done.2, bf16[2,384,384]{2,1,0:T(8,128)(2,1)} %collective-permute-done.1, bf16[24,384,384]{2,1,0:T(8,128)(2,1)} %source_ref.3, ...), kind=kLoop, calls=%fused_computation.9 | loop fusion | flops 62619648 | bytes 17375232 | tf_op jit(solution)/shard_map/concatenate | solution.py:511
  85.5 16.7 %shard_map.124 = (bf16[24,384,384]{2,1,0:T(8,128)(2,1)}, bf16[8,192,384]{2,1,0:T(8,128)(2,1)S(1)}, bf16[8,192,384]{2,1,0:T(8,128)(2,1)S(1)}) custom-call(s32[1]{0:T(128)} %bitcast.place_ref, f32[24,16,128]{2,1,0:T(8,128)S(1)} %pad.26.coef_ref, bf16[28,416,384]{2,1,0:T(8,128)(2,1)} %fusion.5.w0.w1.w2.w3.w4, bf16[28,416,384]{2,1,0:T(8,128)(2,1)} %fusion.5.w0.w1.w2.w3.w4, ...), custom_call_target="tpu_custom_call" | custom-call | flops 9600000000 | bytes 32000000 | tf_op jit(solution)/shard_map/pallas_call | solution.py:219
  122.5 16.7 %shard_map.126 = (bf16[24,384,384]{2,1,0:T(8,128)(2,1)}, bf16[8,192,384]{2,1,0:T(8,128)(2,1)S(1)}, bf16[8,192,384]{2,1,0:T(8,128)(2,1)S(1)}) custom-call(s32[1]{0:T(128)} %bitcast.place_ref, f32[24,16,128]{2,1,0:T(8,128)S(1)} %pad.26.coef_ref, bf16[28,416,384]{2,1,0:T(8,128)(2,1)} %fusion.5.w0.w1.w2.w3.w4, ...), custom_call_target="tpu_custom_call", output_to_operand_aliasing={{0}: (8, {})} | custom-call | flops 9600000000 | bytes 32000000 | tf_op jit(solution)/shard_map/pallas_call | solution.py:219
  141.3 8.3 collective-permute-done.6.refs_1_
  156.5 18.8 %all-to-all-done.1.refs_1_ = bf16[16,24,8,384]{3,2,1,0:T(8,128)(2,1)} async-done(((bf16[16,24,8,384]{3,2,1,0:T(8,128)(2,1)}), bf16[16,24,8,384]{3,2,1,0:T(8,128)(2,1)}, u32[]{:S(2)}, u32[]{:S(2)}) %all-to-all-start.1) | async-done | bytes 2359328 | tf_op jit(solution)/shard_map/all_to_all | solution.py:529
  180.5 27.1 %collective-permute-done.7.refs_1_ = bf16[8,192,384]{2,1,0:T(8,128)(2,1)S(1)} collective-permute-done((bf16[8,192,384]{2,1,0:T(8,128)(2,1)}, bf16[8,192,384]{2,1,0:T(8,128)(2,1)S(1)}, u32[]{:S(2)}, u32[]{:S(2)}) %collective-permute-start.7) | collective-permute-done | bytes 1179680 | tf_op jit(solution)/shard_map/ppermute | solution.py:524
  207.9 16.7 %shard_map.128 = (bf16[24,384,384]{2,1,0:T(8,128)(2,1)}, bf16[8,192,384]{2,1,0:T(8,128)(2,1)S(1)}, bf16[8,192,384]{2,1,0:T(8,128)(2,1)S(1)}) custom-call(s32[1]{0:T(128)} %bitcast.place_ref, f32[24,16,128]{2,1,0:T(8,128)S(1)} %pad.26.coef_ref, bf16[28,416,384]{2,1,0:T(8,128)(2,1)} %fusion.5.w0.w1.w2.w3.w4, ...), custom_call_target="tpu_custom_call", output_to_operand_aliasing={{0}: (8, {})} | custom-call | flops 9600000000 | bytes 32000000 | tf_op jit(solution)/shard_map/pallas_call | solution.py:219
  235.2 8.5 all-to-all-start.3
  244.0 27.1 %collective-permute-done.9.refs_3_ = bf16[8,192,384]{2,1,0:T(8,128)(2,1)S(1)} collective-permute-done((bf16[8,192,384]{2,1,0:T(8,128)(2,1)}, bf16[8,192,384]{2,1,0:T(8,128)(2,1)S(1)}, u32[]{:S(2)}, u32[]{:S(2)}) %collective-permute-start.9) | collective-permute-done | bytes 1179680 | tf_op jit(solution)/shard_map/ppermute | solution.py:524
  275.0 13.4 %shard_map.130 = bf16[16,24,16,384]{3,2,1,0:T(8,128)(2,1)} custom-call(bf16[768,768]{1,0:T(8,128)(2,1)S(1)} %copy.109.table_ref, f32[24,1,384]{2,1,0:T(1,128)S(1)} %broadcast_in_dim.16.quad_ref, bf16[8,192,384]{2,1,0:T(8,128)(2,1)S(1)} %copy-done.22, bf16[8,192,384]{2,1,0:T(8,128)(2,1)S(1)} %copy-done.28, bf16[8,192,384]{2,1,0:T(8,128)(2,1)S(1)} %copy-done.30, ...), custom_call_target="tpu_custom_call" | custom-call | flops 8640000000 | bytes 28800000 | tf_op jit(solution)/shard_map/pallas_call | solution.py:310
  288.4 8.3 all-to-all-done.3.refs_0_
  305.4 74.3 %collective-permute-done.10 = bf16[12,384,384]{2,1,0:T(8,128)(2,1)} collective-permute-done((bf16[12,384,384]{2,1,0:T(8,128)(2,1)}, bf16[12,384,384]{2,1,0:T(8,128)(2,1)}, u32[]{:S(2)}, u32[]{:S(2)}) %collective-permute-start.10) | collective-permute-done | bytes 3538976 | tf_op jit(solution)/shard_map/ppermute | solution.py:524
  385.3 26.0 %shard_map.131 = (bf16[16,24,8,384]{3,2,1,0:T(8,128)(2,1)S(1)}, bf16[16,24,8,384]{3,2,1,0:T(8,128)(2,1)S(1)}, bf16[16,24,8,384]{3,2,1,0:T(8,128)(2,1)}, f32[24,384,384]{2,1,0:T(8,128)}) custom-call(bf16[24,384,384]{2,1,0:T(8,128)(2,1)} %copy-done.43, f32[384,384]{1,0:T(8,128)S(1)} %pad_maximum_fusion.1.gain_ref, f32[384,1]{1,0:T(8,128)S(1)} %sin.19.quad_ref, ...), custom_call_target="tpu_custom_call" | custom-call | flops 15840000000 | bytes 52800000 | tf_op jit(solution)/shard_map/pallas_call | solution.py:437
  420.9 28.7 %shard_map.132 = (bf16[16,24,16,384]{3,2,1,0:T(8,128)(2,1)}, bf16[16,24,8,384]{3,2,1,0:T(8,128)(2,1)S(1)}, f32[384,384]{1,0:T(8,128)S(1)}) custom-call(bf16[24,384,384]{2,1,0:T(8,128)(2,1)} %copy-done.43, f32[384,384]{1,0:T(8,128)S(1)} %pad_maximum_fusion.1.gain_ref, f32[384,1]{1,0:T(8,128)S(1)} %sin.19.quad_ref, ...), custom_call_target="tpu_custom_call" | custom-call | flops 15840000000 | bytes 52800000 | tf_op jit(solution)/shard_map/pallas_call | solution.py:437
  452.0 22.1 %all-to-all-done.5.wide_in_ref = bf16[16,24,8,384]{3,2,1,0:T(8,128)(2,1)} async-done(((bf16[16,24,8,384]{3,2,1,0:T(8,128)(2,1)}), bf16[16,24,8,384]{3,2,1,0:T(8,128)(2,1)}, u32[]{:S(2)}, u32[]{:S(2)}) %all-to-all-start.5) | async-done | bytes 2359328 | tf_op jit(solution)/shard_map/all_to_all | solution.py:529
  488.8 27.0 %collective-permute-done.11.refs_1_ = bf16[8,192,384]{2,1,0:T(8,128)(2,1)S(1)} collective-permute-done((bf16[8,192,384]{2,1,0:T(8,128)(2,1)S(1)}, bf16[8,192,384]{2,1,0:T(8,128)(2,1)S(1)}, u32[]{:S(2)}, u32[]{:S(2)}) %collective-permute-start.11) | collective-permute-done | bytes 1179680 | tf_op jit(solution)/shard_map/ppermute | solution.py:524
  516.8 15.4 %all-to-all-done.6.wide_in_ref = bf16[16,24,8,384]{3,2,1,0:T(8,128)(2,1)} async-done(((bf16[16,24,8,384]{3,2,1,0:T(8,128)(2,1)}), bf16[16,24,8,384]{3,2,1,0:T(8,128)(2,1)}, u32[]{:S(2)}, u32[]{:S(2)}) %all-to-all-start.6) | async-done | bytes 2359328 | tf_op jit(solution)/shard_map/all_to_all | solution.py:529
  554.0 19.3 %collective-permute-done.12.refs_1_ = bf16[8,192,384]{2,1,0:T(8,128)(2,1)S(1)} collective-permute-done((bf16[8,192,384]{2,1,0:T(8,128)(2,1)S(1)}, bf16[8,192,384]{2,1,0:T(8,128)(2,1)S(1)}, u32[]{:S(2)}, u32[]{:S(2)}) %collective-permute-start.12) | collective-permute-done | bytes 1179680 | tf_op jit(solution)/shard_map/ppermute | solution.py:524
  596.6 11.2 %all-to-all-start.8 = ((bf16[16,24,16,384]{3,2,1,0:T(8,128)(2,1)}), bf16[16,24,16,384]{3,2,1,0:T(8,128)(2,1)}, u32[]{:S(2)}, u32[]{:S(2)}) async-start(bf16[16,24,16,384]{3,2,1,0:T(8,128)(2,1)} %get-tuple-element.127), calls=%async_computation.8 | async-start | bytes 9437184 | tf_op jit(solution)/shard_map/all_to_all | solution.py:529
  609.1 8.1 shard_map.137
  620.5 24.0 %collective-permute-done.15.refs_1_ = bf16[8,192,384]{2,1,0:T(8,128)(2,1)} collective-permute-done((bf16[8,192,384]{2,1,0:T(8,128)(2,1)}, bf16[8,192,384]{2,1,0:T(8,128)(2,1)}, u32[]{:S(2)}, u32[]{:S(2)}) %collective-permute-start.15) | collective-permute-done | bytes 1179680 | tf_op jit(solution)/shard_map/ppermute | solution.py:524
  644.5 8.2 shard_map.138
  658.7 13.6 %fusion.7.w0.w1.w2.w3.w4 = bf16[28,416,384]{2,1,0:T(8,128)(2,1)} fusion(bf16[28,4,384]{2,1,0:T(4,128)(2,1)S(1)} %collective-permute-done.17, bf16[28,4,384]{2,1,0:T(4,128)(2,1)S(1)} %collective-permute-done.16, bf16[2,384,384]{2,1,0:T(8,128)(2,1)S(1)} %copy-done.45, bf16[24,384,384]{2,1,0:T(8,128)(2,1)} %shard_map.138, ...), kind=kLoop, calls=%fused_computation.11 | loop fusion | flops 62619648 | bytes 17375232 | tf_op jit(solution)/shard_map/concatenate | solution.py:511
  672.3 39.3 %shard_map.139 = (bf16[24,384,384]{2,1,0:T(8,128)(2,1)}, f32[384,1152]{1,0:T(8,128)S(1)}) custom-call(f32[24,16,128]{2,1,0:T(8,128)S(1)} %pad.29.coef_ref, bf16[28,416,384]{2,1,0:T(8,128)(2,1)} %fusion.7.w0.w1.w2.w3.w4, bf16[28,416,384]{2,1,0:T(8,128)(2,1)} %fusion.7.w0.w1.w2.w3.w4, bf16[28,416,384]{2,1,0:T(8,128)(2,1)} %fusion.7.w0.w1.w2.w3.w4, ...), custom_call_target="tpu_custom_call" | custom-call | flops 23040000000 | bytes 76800000 | tf_op jit(solution)/shard_map/pallas_call | solution.py:248
  721.0 15.2 %shard_map.140 = (bf16[16,192,384]{2,1,0:T(8,128)(2,1)S(1)}, bf16[16,192,384]{2,1,0:T(8,128)(2,1)}) custom-call(bf16[768,768]{1,0:T(8,128)(2,1)S(1)} %copy-done.16, bf16[16,24,16,384]{3,2,1,0:T(8,128)(2,1)} %all-to-all-done.8.wide_in_ref), custom_call_target="tpu_custom_call" | custom-call | flops 7680000000 | bytes 25600000 | tf_op jit(solution)/shard_map/pallas_call | solution.py:362
  738.4 20.5 %shard_map.141 = (bf16[24,384,384]{2,1,0:T(8,128)(2,1)}, f32[384,1152]{1,0:T(8,128)S(1)}) custom-call(f32[24,16,128]{2,1,0:T(8,128)S(1)} %pad.29.coef_ref, bf16[28,416,384]{2,1,0:T(8,128)(2,1)} %fusion.7.w0.w1.w2.w3.w4, bf16[28,416,384]{2,1,0:T(8,128)(2,1)} %fusion.7.w0.w1.w2.w3.w4, ...), custom_call_target="tpu_custom_call", output_to_operand_aliasing={{0}: (8, {})} | custom-call | flops 11520000000 | bytes 38400000 | tf_op jit(solution)/shard_map/pallas_call | solution.py:248
  760.0 14.2 %all-to-all-done.9.wide_in_ref = bf16[16,24,8,384]{3,2,1,0:T(8,128)(2,1)} async-done(((bf16[16,24,8,384]{3,2,1,0:T(8,128)(2,1)}), bf16[16,24,8,384]{3,2,1,0:T(8,128)(2,1)}, u32[]{:S(2)}, u32[]{:S(2)}) %all-to-all-start.9) | async-done | bytes 2359328 | tf_op jit(solution)/shard_map/all_to_all | solution.py:529
  779.1 8.1 shard_map.142
  791.1 13.9 %all-to-all-done.10 = bf16[16,24,1344]{2,1,0:T(8,128)(2,1)} async-done(((bf16[16,24,1344]{2,1,0:T(8,128)(2,1)}), bf16[16,24,1344]{2,1,0:T(8,128)(2,1)}, u32[]{:S(2)}, u32[]{:S(2)}) %all-to-all-start.10) | async-done | bytes 1032224 | tf_op jit(solution)/shard_map/all_to_all | solution.py:529
  807.1 12.8 %collective-permute-done.20 = f32[24,1344]{1,0:T(8,128)S(1)} collective-permute-done((f32[24,1344]{1,0:T(8,128)S(1)}, f32[24,1344]{1,0:T(8,128)S(1)}, u32[]{:S(2)}, u32[]{:S(2)}) %collective-permute-start.20) | collective-permute-done | bytes 129056 | tf_op jit(solution)/shard_map/ppermute | solution.py:524
  831.3 12.9 %shard_map.143.refs_2_ = bf16[24,384,384]{2,1,0:T(8,128)(2,1)} custom-call(s32[1]{0:T(128)} %bitcast.place_ref, bf16[24,384,384]{2,1,0:T(8,128)(2,1)} %get-tuple-element.93.conv_ref, bf16[16,192,384]{2,1,0:T(8,128)(2,1)S(1)} %copy-done.39, bf16[16,192,384]{2,1,0:T(8,128)(2,1)} %collective-permute-done.18.refs_1_), custom_call_target="tpu_custom_call" | custom-call | flops 8640000000 | bytes 28800000 | tf_op jit(solution)/shard_map/pallas_call | solution.py:475
  (242 shorter events, 264.2 us)
Async XLA Ops:
  3.1 53.9 %collective-permute-start = (bf16[2,384,384]{2,1,0:T(8,128)(2,1)}, bf16[2,384,384]{2,1,0:T(8,128)(2,1)}, u32[]{:S(2)}, u32[]{:S(2)}) collective-permute-start(bf16[2,384,384]{2,1,0:T(8,128)(2,1)} %get-tuple-element.172), channel_id=1, source_target_pairs={{0,2},{2,4},{4,6},{6,8},{8,10},{10,12},{12,14},{14,16},{16,18},{18... | collective-permute-start | bytes 1769480 | tf_op jit(solution)/shard_map/ppermute | solution.py:495
  6.8 50.2 %collective-permute-start.1 = (bf16[2,384,384]{2,1,0:T(8,128)(2,1)}, bf16[2,384,384]{2,1,0:T(8,128)(2,1)}, u32[]{:S(2)}, u32[]{:S(2)}) collective-permute-start(bf16[2,384,384]{2,1,0:T(8,128)(2,1)} %get-tuple-element.173), channel_id=1, source_target_pairs={{2,0},{4,2},{6,4},{8,6},{10,8},{12,10},{14,12},{16,14},{18,16},{20... | collective-permute-start | bytes 1769480 | tf_op jit(solution)/shard_map/ppermute | solution.py:496
  16.0 32.3 %collective-permute-start.3 = (bf16[8,192,384]{2,1,0:T(8,128)(2,1)}, bf16[8,192,384]{2,1,0:T(8,128)(2,1)}, u32[]{:S(2)}, u32[]{:S(2)}) collective-permute-start(bf16[8,192,384]{2,1,0:T(8,128)(2,1)} %get-tuple-element.80), channel_id=1, source_target_pairs={{0,1},{1,0},{2,3},{3,2},{4,5},{5,4},{6,7},{7,6},{8,9},{9,8},{10,11... | collective-permute-start | bytes 3538952 | tf_op jit(solution)/shard_map/ppermute | solution.py:524
  57.0 60.2 %all-to-all-start = ((bf16[16,24,8,384]{3,2,1,0:T(8,128)(2,1)}), bf16[16,24,8,384]{3,2,1,0:T(8,128)(2,1)}, u32[]{:S(2)}, u32[]{:S(2)}) async-start(bf16[16,24,8,384]{3,2,1,0:T(8,128)(2,1)} %shard_map.123), calls=%async_computation | async-start | bytes 4718592 | tf_op jit(solution)/shard_map/all_to_all | solution.py:529
  65.9 3.9 collective-permute-start.2
  66.2 5.4 collective-permute-start.4
  68.6 35.7 %collective-permute-start.5 = (bf16[8,192,384]{2,1,0:T(8,128)(2,1)}, bf16[8,192,384]{2,1,0:T(8,128)(2,1)S(1)}, u32[]{:S(2)}, u32[]{:S(2)}) collective-permute-start(bf16[8,192,384]{2,1,0:T(8,128)(2,1)} %copy-done.20), channel_id=1, source_target_pairs={{0,1},{1,0},{2,3},{3,2},{4,5},{5,4},{6,7},{7,6},{8,9},{9,8},{10,11... | collective-permute-start | bytes 3538952 | tf_op jit(solution)/shard_map/ppermute | solution.py:524
  117.3 58.0 %all-to-all-start.1 = ((bf16[16,24,8,384]{3,2,1,0:T(8,128)(2,1)}), bf16[16,24,8,384]{3,2,1,0:T(8,128)(2,1)}, u32[]{:S(2)}, u32[]{:S(2)}) async-start(bf16[16,24,8,384]{3,2,1,0:T(8,128)(2,1)} %copy-done.7), calls=%async_computation.1 | async-start | bytes 4718592 | tf_op jit(solution)/shard_map/all_to_all | solution.py:529
  122.1 27.5 %collective-permute-start.6 = (bf16[8,192,384]{2,1,0:T(8,128)(2,1)}, bf16[8,192,384]{2,1,0:T(8,128)(2,1)S(1)}, u32[]{:S(2)}, u32[]{:S(2)}) collective-permute-start(bf16[8,192,384]{2,1,0:T(8,128)(2,1)} %copy-done.19), channel_id=1, source_target_pairs={{0,1},{1,0},{2,3},{3,2},{4,5},{5,4},{6,7},{7,6},{8,9},{9,8},{10,11... | collective-permute-start | bytes 3538952 | tf_op jit(solution)/shard_map/ppermute | solution.py:524
  175.3 59.9 %all-to-all-start.2 = ((bf16[16,24,8,384]{3,2,1,0:T(8,128)(2,1)}), bf16[16,24,8,384]{3,2,1,0:T(8,128)(2,1)}, u32[]{:S(2)}, u32[]{:S(2)}) async-start(bf16[16,24,8,384]{3,2,1,0:T(8,128)(2,1)} %copy-done.5), calls=%async_computation.2 | async-start | bytes 4718592 | tf_op jit(solution)/shard_map/all_to_all | solution.py:529
  180.2 27.4 %collective-permute-start.7 = (bf16[8,192,384]{2,1,0:T(8,128)(2,1)}, bf16[8,192,384]{2,1,0:T(8,128)(2,1)S(1)}, u32[]{:S(2)}, u32[]{:S(2)}) collective-permute-start(bf16[8,192,384]{2,1,0:T(8,128)(2,1)} %copy-done.25), channel_id=1, source_target_pairs={{0,1},{1,0},{2,3},{3,2},{4,5},{5,4},{6,7},{7,6},{8,9},{9,8},{10,11... | collective-permute-start | bytes 3538952 | tf_op jit(solution)/shard_map/ppermute | solution.py:524
  207.6 26.5 %collective-permute-start.8 = (bf16[8,192,384]{2,1,0:T(8,128)(2,1)}, bf16[8,192,384]{2,1,0:T(8,128)(2,1)S(1)}, u32[]{:S(2)}, u32[]{:S(2)}) collective-permute-start(bf16[8,192,384]{2,1,0:T(8,128)(2,1)} %copy-done.26), channel_id=1, source_target_pairs={{0,1},{1,0},{2,3},{3,2},{4,5},{5,4},{6,7},{7,6},{8,9},{9,8},{10,11... | collective-permute-start | bytes 3538952 | tf_op jit(solution)/shard_map/ppermute | solution.py:524
  235.2 61.5 %all-to-all-start.3 = ((bf16[16,24,8,384]{3,2,1,0:T(8,128)(2,1)}), bf16[16,24,8,384]{3,2,1,0:T(8,128)(2,1)}, u32[]{:S(2)}, u32[]{:S(2)}) async-start(bf16[16,24,8,384]{3,2,1,0:T(8,128)(2,1)} %copy-done.6), calls=%async_computation.3 | async-start | bytes 4718592 | tf_op jit(solution)/shard_map/all_to_all | solution.py:529
  243.7 27.5 %collective-permute-start.9 = (bf16[8,192,384]{2,1,0:T(8,128)(2,1)}, bf16[8,192,384]{2,1,0:T(8,128)(2,1)S(1)}, u32[]{:S(2)}, u32[]{:S(2)}) collective-permute-start(bf16[8,192,384]{2,1,0:T(8,128)(2,1)} %copy-done.31), channel_id=1, source_target_pairs={{0,1},{1,0},{2,3},{3,2},{4,5},{5,4},{6,7},{7,6},{8,9},{9,8},{10,11... | collective-permute-start | bytes 3538952 | tf_op jit(solution)/shard_map/ppermute | solution.py:524
  296.7 117.4 %all-to-all-start.4 = ((bf16[16,24,16,384]{3,2,1,0:T(8,128)(2,1)}), bf16[16,24,16,384]{3,2,1,0:T(8,128)(2,1)}, u32[]{:S(2)}, u32[]{:S(2)}) async-start(bf16[16,24,16,384]{3,2,1,0:T(8,128)(2,1)} %shard_map.130), calls=%async_computation.4 | async-start | bytes 9437184 | tf_op jit(solution)/shard_map/all_to_all | solution.py:529
  301.6 78.1 %collective-permute-start.10 = (bf16[12,384,384]{2,1,0:T(8,128)(2,1)}, bf16[12,384,384]{2,1,0:T(8,128)(2,1)}, u32[]{:S(2)}, u32[]{:S(2)}) collective-permute-start(bf16[12,384,384]{2,1,0:T(8,128)(2,1)} %param.13), channel_id=1, source_target_pairs={{0,1},{1,0},{2,3},{3,2},{4,5},{5,4},{6,7},{7,6},{8,9},{9,8},{10,11... | collective-permute-start | bytes 10616840 | tf_op jit(solution)/shard_map/ppermute | solution.py:524
  414.1 60.0 %all-to-all-start.5 = ((bf16[16,24,8,384]{3,2,1,0:T(8,128)(2,1)}), bf16[16,24,8,384]{3,2,1,0:T(8,128)(2,1)}, u32[]{:S(2)}, u32[]{:S(2)}) async-start(bf16[16,24,8,384]{3,2,1,0:T(8,128)(2,1)} %copy-done.8), calls=%async_computation.5 | async-start | bytes 4718592 | tf_op jit(solution)/shard_map/all_to_all | solution.py:529
  474.1 58.2 %all-to-all-start.6 = ((bf16[16,24,8,384]{3,2,1,0:T(8,128)(2,1)}), bf16[16,24,8,384]{3,2,1,0:T(8,128)(2,1)}, u32[]{:S(2)}, u32[]{:S(2)}) async-start(bf16[16,24,8,384]{3,2,1,0:T(8,128)(2,1)} %get-tuple-element.118), calls=%async_computation.6 | async-start | bytes 4718592 | tf_op jit(solution)/shard_map/all_to_all | solution.py:529
  488.5 27.4 %collective-permute-start.11 = (bf16[8,192,384]{2,1,0:T(8,128)(2,1)S(1)}, bf16[8,192,384]{2,1,0:T(8,128)(2,1)S(1)}, u32[]{:S(2)}, u32[]{:S(2)}) collective-permute-start(bf16[8,192,384]{2,1,0:T(8,128)(2,1)S(1)} %get-tuple-element.120), channel_id=1, source_target_pairs={{0,1},{1,0},{2,3},{3,2},{4,5},{5,4},{6,7},{7,6},{8,9},{9,8},{10,11... | collective-permute-start | bytes 3538952 | tf_op jit(solution)/shard_map/ppermute | solution.py:524
  532.3 64.3 %all-to-all-start.7 = ((bf16[16,24,8,384]{3,2,1,0:T(8,128)(2,1)}), bf16[16,24,8,384]{3,2,1,0:T(8,128)(2,1)}, u32[]{:S(2)}, u32[]{:S(2)}) async-start(bf16[16,24,8,384]{3,2,1,0:T(8,128)(2,1)} %copy-done.4), calls=%async_computation.7 | async-start | bytes 4718592 | tf_op jit(solution)/shard_map/all_to_all | solution.py:529
  545.9 27.4 %collective-permute-start.12 = (bf16[8,192,384]{2,1,0:T(8,128)(2,1)S(1)}, bf16[8,192,384]{2,1,0:T(8,128)(2,1)S(1)}, u32[]{:S(2)}, u32[]{:S(2)}) collective-permute-start(bf16[8,192,384]{2,1,0:T(8,128)(2,1)S(1)} %get-tuple-element.124), channel_id=1, source_target_pairs={{0,1},{1,0},{2,3},{3,2},{4,5},{5,4},{6,7},{7,6},{8,9},{9,8},{10,11... | collective-permute-start | bytes 3538952 | tf_op jit(solution)/shard_map/ppermute | solution.py:524
  582.4 14.2 %collective-permute-start.14 = (bf16[2,384,384]{2,1,0:T(8,128)(2,1)S(1)}, bf16[2,384,384]{2,1,0:T(8,128)(2,1)S(1)}, u32[]{:S(2)}, u32[]{:S(2)}) collective-permute-start(bf16[2,384,384]{2,1,0:T(8,128)(2,1)S(1)} %get-tuple-element.170), channel_id=1, source_target_pairs={{2,0},{4,2},{6,4},{8,6},{10,8},{12,10},{14,12},{16,14},{18,16},{20... | collective-permute-start | bytes 1769480 | tf_op jit(solution)/shard_map/ppermute | solution.py:496
  585.4 11.2 %collective-permute-start.13 = (bf16[2,384,384]{2,1,0:T(8,128)(2,1)S(1)}, bf16[2,384,384]{2,1,0:T(8,128)(2,1)}, u32[]{:S(2)}, u32[]{:S(2)}) collective-permute-start(bf16[2,384,384]{2,1,0:T(8,128)(2,1)S(1)} %get-tuple-element.171), channel_id=1, source_target_pairs={{0,2},{2,4},{4,6},{6,8},{8,10},{10,12},{12,14},{14,16},{16,18},{18... | collective-permute-start | bytes 1769480 | tf_op jit(solution)/shard_map/ppermute | solution.py:495
  596.6 116.2 %all-to-all-start.8 = ((bf16[16,24,16,384]{3,2,1,0:T(8,128)(2,1)}), bf16[16,24,16,384]{3,2,1,0:T(8,128)(2,1)}, u32[]{:S(2)}, u32[]{:S(2)}) async-start(bf16[16,24,16,384]{3,2,1,0:T(8,128)(2,1)} %get-tuple-element.127), calls=%async_computation.8 | async-start | bytes 9437184 | tf_op jit(solution)/shard_map/all_to_all | solution.py:529
  617.1 27.4 %collective-permute-start.15 = (bf16[8,192,384]{2,1,0:T(8,128)(2,1)}, bf16[8,192,384]{2,1,0:T(8,128)(2,1)}, u32[]{:S(2)}, u32[]{:S(2)}) collective-permute-start(bf16[8,192,384]{2,1,0:T(8,128)(2,1)} %get-tuple-element.131), channel_id=1, source_target_pairs={{0,1},{1,0},{2,3},{3,2},{4,5},{5,4},{6,7},{7,6},{8,9},{9,8},{10,11... | collective-permute-start | bytes 3538952 | tf_op jit(solution)/shard_map/ppermute | solution.py:524
  654.3 4.4 collective-permute-start.17
  712.8 61.5 %all-to-all-start.9 = ((bf16[16,24,8,384]{3,2,1,0:T(8,128)(2,1)}), bf16[16,24,8,384]{3,2,1,0:T(8,128)(2,1)}, u32[]{:S(2)}, u32[]{:S(2)}) async-start(bf16[16,24,8,384]{3,2,1,0:T(8,128)(2,1)} %copy-done.3), calls=%async_computation.9 | async-start | bytes 4718592 | tf_op jit(solution)/shard_map/all_to_all | solution.py:529
  737.7 52.8 %collective-permute-start.18 = (bf16[16,192,384]{2,1,0:T(8,128)(2,1)}, bf16[16,192,384]{2,1,0:T(8,128)(2,1)}, u32[]{:S(2)}, u32[]{:S(2)}) collective-permute-start(bf16[16,192,384]{2,1,0:T(8,128)(2,1)} %get-tuple-element.142), channel_id=1, source_target_pairs={{0,1},{1,0},{2,3},{3,2},{4,5},{5,4},{6,7},{7,6},{8,9},{9,8},{10,11... | collective-permute-start | bytes 7077896 | tf_op jit(solution)/shard_map/ppermute | solution.py:524
  774.2 30.8 %all-to-all-start.10 = ((bf16[16,24,1344]{2,1,0:T(8,128)(2,1)}), bf16[16,24,1344]{2,1,0:T(8,128)(2,1)}, u32[]{:S(2)}, u32[]{:S(2)}) async-start(bf16[16,24,1344]{2,1,0:T(8,128)(2,1)} %pad_maximum_fusion), calls=%async_computation.10 | async-start | bytes 2162688 | tf_op jit(solution)/shard_map/all_to_all | solution.py:529
  790.5 30.2 %collective-permute-start.19 = (bf16[8,192,384]{2,1,0:T(8,128)(2,1)}, bf16[8,192,384]{2,1,0:T(8,128)(2,1)S(1)}, u32[]{:S(2)}, u32[]{:S(2)}) collective-permute-start(bf16[8,192,384]{2,1,0:T(8,128)(2,1)} %get-tuple-element.143), channel_id=1, source_target_pairs={{0,1},{1,0},{2,3},{3,2},{4,5},{5,4},{6,7},{7,6},{8,9},{9,8},{10,11... | collective-permute-start | bytes 3538952 | tf_op jit(solution)/shard_map/ppermute | solution.py:524
  806.4 13.5 %collective-permute-start.20 = (f32[24,1344]{1,0:T(8,128)S(1)}, f32[24,1344]{1,0:T(8,128)S(1)}, u32[]{:S(2)}, u32[]{:S(2)}) collective-permute-start(f32[24,1344]{1,0:T(8,128)S(1)} %convert_reduce_fusion), channel_id=1, source_target_pairs={{0,1},{1,0},{2,3},{3,2},{4,5},{5,4},{6,7},{7,6},{8,9},{9,8},{10,11... | collective-permute-start | bytes 387080 | tf_op jit(solution)/shard_map/ppermute | solution.py:524
  821.8 35.6 %all-to-all-start.11 = ((bf16[16,24,1536]{2,1,0:T(8,128)(2,1)}), bf16[16,24,1536]{2,1,0:T(8,128)(2,1)}, u32[]{:S(2)}, u32[]{:S(2)}) async-start(bf16[16,24,1536]{2,1,0:T(8,128)(2,1)} %broadcast_in_dim.17), calls=%async_computation.11 | async-start | bytes 2359296 | tf_op jit(solution)/shard_map/all_to_all | solution.py:529
  (54 other events, 557.9 us)
